TPU v7x, 256 devices: a whole 4x4x8 slice. The times are simulated.
256 devices in a mesh: section: 2 (over core), expert: 128 (over x, z, y).
Axes of the slice: x: 4, y: 4, z: 8, core: 2. Of those that a mesh axis runs over, the one named last changes fastest.
Arguments:
- arriving: bfloat16 [2, 8192, 7168], P('section', 'expert'), may hold values from -6 to 6
- gains: float32 [2, 7168], P('section'), may hold values from 0.5 to 2
- routes: int32 [2, 8192, 3], P('section', 'expert'), may hold values from 0 to 31, all different within a row; in each aligned block of 64 rows (0 to 63, 64 to 127, ..., all dimensions but the last counted through in order) at most 7 rows name the same one
- combine_weight: float32 [2, 8192, 3], P('section', 'expert'), may hold values from 0.2 to 1
- gate_weight: bfloat16 [2, 7168, 32768], P('section', None, 'expert'), may hold values from -0.0625 to 0.0625
- up_weight: bfloat16 [2, 7168, 32768], P('section', None, 'expert'), may hold values from -0.0625 to 0.0625
- down_weight: bfloat16 [2, 32768, 7168], P('section', 'expert'), may hold values from -0.1875 to 0.1875
Outputs:
- moved: bfloat16 [2, 8192, 7168], P('section', 'expert')
Inputs may be any that keep to these rules, and one draw needn't show every extreme that they name: `routes`: A token names 3 different experts. Among the tokens of one device (aligned blocks of 64 rows), no expert is named by more than 7 of them, and in every draw some expert is named by exactly 7 of them in some device's rows.
All inputs are finite; a program needn't handle non-finite values.
Results may differ from a plain program's by a relative error of at most 0.0095.
Values may be sent and summed in bfloat16 or wider, within the bound.
No kernel may reach another device: no remote copies, remote signals or barrier semaphores. Data moves between devices by JAX's collectives and lax.ppermute only.
A program may use at most 128 MiB of HBM per device.

v0:
```python
import functools

import jax
import jax.numpy as jnp
from jax import lax
from jax.experimental import pallas as pl
from jax.experimental.pallas import tpu as pltpu
from jax.sharding import PartitionSpec as P

FF_WIN = 1024
HID_DEV = 256
CHUNKS = 2
PAD = 8

epsilon = 1e-06


def gate_up_kernel(pieces, steps, last, *refs):
    piece_refs = refs[:pieces]
    gate_ref, up_ref = refs[pieces : pieces + 2]
    rest = refs[pieces + 2 :]
    start_refs, out_ref, acc_ref = rest[:-2], rest[-2], rest[-1]
    step = pl.program_id(0)

    @pl.when(step == 0)
    def _():
        if start_refs:
            acc_ref[...] = start_refs[0][...]
        else:
            acc_ref[...] = jnp.zeros_like(acc_ref)

    rows = jnp.concatenate([ref[...] for ref in piece_refs], axis=0)
    hid = gate_ref.shape[1]
    acc_ref[:, :hid] += jnp.dot(rows, gate_ref[...], preferred_element_type=jnp.float32)
    acc_ref[:, hid:] += jnp.dot(rows, up_ref[...], preferred_element_type=jnp.float32)

    @pl.when(step == steps - 1)
    def _():
        if last:
            gate = acc_ref[:, :hid]
            out_ref[...] = (gate / (1.0 + jnp.exp(-gate)) * acc_ref[:, hid:]).astype(out_ref.dtype)
        else:
            out_ref[...] = acc_ref[...]


def gate_up(pieces, gate_weight, up_weight, first_row, before, last):
    piece_rows, width = pieces[0].shape
    depth = 512
    steps = width // depth
    offset = first_row // depth
    rows = piece_rows * len(pieces)
    hid = gate_weight.shape[1]
    start = [] if before is None else [before]
    out_shape = (rows, hid) if last else (rows, 2 * hid)
    out_type = jnp.bfloat16 if last else jnp.float32
    return pl.pallas_call(
        functools.partial(gate_up_kernel, len(pieces), steps, last),
        grid=(steps,),
        in_specs=[pl.BlockSpec((piece_rows, depth), lambda k: (0, k)) for _ in pieces]
        + [pl.BlockSpec((depth, hid), lambda k: (k + offset, 0))] * 2
        + [pl.BlockSpec((rows, 2 * hid), lambda k: (0, 0)) for _ in start],
        out_specs=pl.BlockSpec(out_shape, lambda k: (0, 0)),
        out_shape=jax.ShapeDtypeStruct(out_shape, out_type),
        scratch_shapes=[pltpu.VMEM((rows, 2 * hid), jnp.float32)],
        compiler_params=pltpu.CompilerParams(vmem_limit_bytes=40 << 20),
        cost_estimate=pl.CostEstimate(
            flops=4 * rows * hid * width, bytes_accessed=2 * (rows + 2 * hid) * width, transcendentals=0
        ),
        name="gate_up",
    )(*pieces, gate_weight, up_weight, *start)


def down_kernel(orders, *refs):
    parts = len(orders)
    hid_refs, weight_refs = refs[:parts], refs[parts : 2 * parts]
    spread_ref, out_ref, spread_hid = refs[2 * parts :]
    hid = hid_refs[0].shape[1]
    block = hid_refs[0].shape[0] // parts

    @pl.when(pl.program_id(0) == 0)
    def _():
        for j in range(parts):
            rows = jnp.concatenate(
                [hid_refs[j][b * block : (b + 1) * block, :] for b in orders[j]], axis=0
            )
            spread_hid[:, j * hid : (j + 1) * hid] = jnp.dot(
                spread_ref[...], rows, preferred_element_type=jnp.float32
            ).astype(spread_hid.dtype)

    weights = jnp.concatenate([ref[...] for ref in weight_refs], axis=0)
    out_ref[...] = jnp.dot(spread_hid[...], weights, preferred_element_type=jnp.float32).astype(
        out_ref.dtype
    )


def down(hiddens, weights, spread, orders):
    rows, hid = hiddens[0].shape
    out_rows, width = spread.shape[0], weights[0].shape[1]
    cols = 896
    parts = len(orders)
    return pl.pallas_call(
        functools.partial(down_kernel, orders),
        grid=(width // cols,),
        in_specs=[pl.BlockSpec((rows, hid), lambda n: (0, 0))] * parts
        + [pl.BlockSpec((hid, cols), lambda n: (0, n))] * parts
        + [pl.BlockSpec(spread.shape, lambda n: (0, 0))],
        out_specs=pl.BlockSpec((out_rows, cols), lambda n: (0, n)),
        out_shape=jax.ShapeDtypeStruct((out_rows, width), jnp.bfloat16),
        scratch_shapes=[pltpu.VMEM((out_rows, parts * hid), jnp.bfloat16)],
        compiler_params=pltpu.CompilerParams(vmem_limit_bytes=40 << 20),
        cost_estimate=pl.CostEstimate(
            flops=2 * out_rows * parts * hid * (width + rows),
            bytes_accessed=2 * (out_rows + parts * hid) * width,
            transcendentals=0,
        ),
        name="down",
    )(*hiddens, *weights, spread)


def mix_kernel(parts, width, returned_ref, mixing_ref, inbound_ref, out_ref):
    tokens = inbound_ref.shape[0]
    cols = returned_ref.shape[1]
    start = pl.program_id(0) * cols
    product = jnp.dot(mixing_ref[...], returned_ref[...], preferred_element_type=jnp.float32)
    for f in range(parts):
        at = pl.ds(pl.multiple_of(f * width + start, 128), cols)
        high = product[f * tokens : (f + 1) * tokens]
        low = product[(parts + f) * tokens : (parts + f + 1) * tokens]
        total = inbound_ref[:, at].astype(jnp.float32) + (high + low)
        out_ref[:, at] = total.astype(out_ref.dtype)


def mix(returned, mixing, inbound, parts):
    rows, width = returned.shape
    cols = 256
    return pl.pallas_call(
        functools.partial(mix_kernel, parts, width),
        grid=(width // cols,),
        in_specs=[
            pl.BlockSpec((rows, cols), lambda n: (0, n)),
            pl.BlockSpec(mixing.shape, lambda n: (0, 0)),
            pl.BlockSpec(inbound.shape, lambda n: (0, 0)),
        ],
        out_specs=pl.BlockSpec(inbound.shape, lambda n: (0, 0)),
        out_shape=jax.ShapeDtypeStruct(inbound.shape, inbound.dtype),
        compiler_params=pltpu.CompilerParams(vmem_limit_bytes=40 << 20),
        name="mix",
    )(returned, mixing, inbound)


def body(arriving, gains, routes, combine_weight, gate_weight, up_weight, down_weight):
    device_count = lax.axis_size("expert")
    ring = FF_WIN // HID_DEV
    experts = device_count // ring
    tok_count = arriving.shape[1]
    feature_count = arriving.shape[2]
    top_count = routes.shape[2]
    capacity = min(tok_count, 5 * tok_count * top_count // (4 * experts))
    slots = experts * capacity
    padded = experts * PAD
    half = slots // 2
    width = feature_count // CHUNKS
    quarter = feature_count // ring
    planes = [[g * ring + r for g in range(experts)] for r in range(ring)]
    place = lax.rem(lax.axis_index("expert"), ring)

    def shift(block, step):
        route = [(i, i - i % ring + (i + step) % ring) for i in range(device_count)]
        return lax.ppermute(block, "expert", route)

    def exchange(block, groups):
        return lax.all_to_all(
            block, "expert", split_axis=0, concat_axis=0, axis_index_groups=groups, tiled=True
        )

    def weight_part(step):
        start = lax.rem(place + step, ring) * quarter
        return lax.dynamic_slice_in_dim(down_weight[0], start, quarter, 1)

    other = [(i, 1 - i) for i in range(2)]
    inbound = lax.ppermute(arriving, "section", other)[0]
    down_parts = [
        weight_part(0),
        shift(weight_part(1), 1),
        shift(weight_part(3), -1),
        shift(weight_part(2), 2),
    ]
    widened = inbound.astype(jnp.float32)
    inv_rms = lax.rsqrt(jnp.mean(widened * widened, axis=-1, keepdims=True) + epsilon)
    normed = (widened * inv_rms * gains[0][None, :]).astype(jnp.bfloat16)
    chosen = routes[0].reshape(-1)
    onehot = (chosen[:, None] == jnp.arange(experts, dtype=jnp.int32)[None, :]).astype(jnp.int32)
    earlier = jnp.cumsum(onehot, axis=0) - onehot
    slot_index = jnp.sum(earlier * onehot, axis=1)
    target = (chosen * PAD + slot_index).reshape(tok_count, top_count)
    slot_ids = jnp.arange(padded, dtype=jnp.int32)
    hits = target[:, :, None] == slot_ids[None, None, :]
    placement = jnp.any(hits, axis=1).astype(jnp.bfloat16).T

    def rows_of(count, size):
        ids = jnp.arange(count * size, dtype=jnp.int32)
        return ids // size, ids % size

    to_block, to_slot = rows_of(experts // 2, capacity)
    from_block, from_slot = rows_of(experts // 2, PAD)
    squeeze = (to_block * PAD + to_slot)[:, None] == (from_block * PAD + from_slot)[None, :]
    squeeze = squeeze.astype(jnp.bfloat16)

    def squeezed(block):
        return jnp.dot(squeeze, block, preferred_element_type=jnp.float32).astype(jnp.bfloat16)

    packed = [
        jnp.dot(placement, normed[:, c * width : (c + 1) * width], preferred_element_type=jnp.float32)
        .astype(jnp.bfloat16)
        .reshape(experts, PAD, width)
        for c in range(CHUNKS)
    ]
    state = None
    for c in range(CHUNKS):
        landed = exchange(packed[c], planes).reshape(padded, width)
        if c == 0:
            landed, *down_parts = lax.optimization_barrier((landed, *down_parts))
        first, second = squeezed(landed[: padded // 2]), squeezed(landed[padded // 2 :])
        if c + 1 < CHUNKS:
            first, second, packed[c + 1] = lax.optimization_barrier((first, second, packed[c + 1]))
        left_first, right_second = shift(first, 1), shift(second, -1)
        left_second, right_first = shift(second, 1), shift(first, -1)
        far_first, far_second = shift(left_first, 1), shift(right_second, -1)
        pieces = [
            first, second, left_first, left_second, right_first, right_second, far_first, far_second
        ]
        state = gate_up(
            pieces, gate_weight[0], up_weight[0], c * width, state, c == CHUNKS - 1
        )
    hiddens = [state, shift(state, 1), shift(state, -1), shift(state, 2)]
    orders = ((0, 1, 2, 3), (2, 0, 3, 1), (1, 3, 0, 2), (3, 2, 1, 0))

    row = jnp.arange(device_count * PAD, dtype=jnp.int32)
    column = jnp.arange(ring * slots, dtype=jnp.int32)
    relative = column // slots
    away = jnp.where(relative == 1, ring - 1, jnp.where(relative == 2, 1, jnp.where(relative == 3, 2, 0)))
    origin = lax.rem(place + away, jnp.int32(ring))
    inner = column % slots
    goal = (inner // capacity * ring + origin) * PAD + inner % capacity
    spread = (row[:, None] == goal[None, :]).astype(jnp.bfloat16)
    complete = down(hiddens, down_parts, spread, orders)
    returned = exchange(complete.reshape(device_count, PAD, quarter), None)
    returned = returned.reshape(device_count * PAD, quarter)

    mixing = jnp.sum(jnp.where(hits, combine_weight[0][:, :, None], 0.0), axis=1)
    mix_high = lax.reduce_precision(mixing, 8, 7)
    both = jnp.stack([mix_high, mixing - mix_high]).astype(jnp.bfloat16)
    both = both.reshape(2, 1, tok_count, experts, 1, PAD)
    same = jnp.arange(ring)[:, None] == jnp.arange(ring)[None, :]
    both = jnp.where(same[None, :, None, None, :, None], both, jnp.bfloat16(0))
    both = both.reshape(2 * ring * tok_count, device_count * PAD)
    return mix(returned, both, inbound, ring)[None]


def solution(mesh):
    placed = (
        P("section", "expert", None),
        P("section", None),
        P("section", "expert", None),
        P("section", "expert", None),
        P("section", None, "expert"),
        P("section", None, "expert"),
        P("section", "expert", None),
    )
    return jax.shard_map(
        body, mesh=mesh, in_specs=placed, out_specs=P("section", "expert", None), check_vma=False
    )
```

profile of v0, /device:TPU:32, one launch (start us, length us, event | category | flops | bytes accessed | tf_op | source)
XLA Modules:
  0.0 332.4 jit_solution(8633291328546585641)
XLA Ops:
  3.0 1.0 fusion.5
  4.0 1.9 fusion
  5.9 11.2 %all-to-all-start = ((bf16[32,8,3584]{2,1,0:T(8,128)(2,1)}), bf16[32,8,3584]{2,1,0:T(8,128)(2,1)}, u32[]{:S(2)}, u32[]{:S(2)}) async-start(bf16[32,8,3584]{2,1,0:T(8,128)(2,1)} %fusion), calls=%async_computation | async-start | bytes 3670016 | tf_op jit(solution)/shard_map/all_to_all | solution.py:172
  17.2 2.3 dynamic-slice_bitcast_fusion
  19.5 1.7 collective-permute-start.1
  21.1 1.7 collective-permute-start.2
  22.8 2.0 collective-permute-start.3
  24.8 1.9 fusion.1
  26.7 16.2 %collective-permute-done.1.refs_5_ = bf16[256,1792]{1,0:T(8,128)(2,1)S(1)} collective-permute-done((bf16[256,1792]{1,0:T(8,128)(2,1)S(1)}, bf16[256,1792]{1,0:T(8,128)(2,1)S(1)}, u32[]{:S(2)}, u32[]{:S(2)}) %collective-permute-start.1) | collective-permute-done | bytes 917536 | tf_op jit(solution)/shard_map/ppermute | solution.py:169
  42.9 0.9 copy-done.3
  43.9 17.9 %collective-permute-done.2.refs_6_ = bf16[256,1792]{1,0:T(8,128)(2,1)S(1)} collective-permute-done((bf16[256,1792]{1,0:T(8,128)(2,1)S(1)}, bf16[256,1792]{1,0:T(8,128)(2,1)S(1)}, u32[]{:S(2)}, u32[]{:S(2)}) %collective-permute-start.2) | collective-permute-done | bytes 917536 | tf_op jit(solution)/shard_map/ppermute | solution.py:169
  61.7 0.9 copy-done.5
  62.6 0.9 collective-permute-done.3.refs_7_
  63.5 1.0 copy-done.7
  64.5 1.6 convolution_convert_fusion.4.refs_1_
  66.1 1.6 convolution_convert_fusion.5.refs_0_
  67.7 9.8 %all-to-all-start.1 = ((bf16[32,8,3584]{2,1,0:T(8,128)(2,1)}), bf16[32,8,3584]{2,1,0:T(8,128)(2,1)}, u32[]{:S(2)}, u32[]{:S(2)}) async-start(bf16[32,8,3584]{2,1,0:T(8,128)(2,1)} %fusion.1), calls=%async_computation.1 | async-start | bytes 3670016 | tf_op jit(solution)/shard_map/all_to_all | solution.py:172
  77.6 1.2 collective-permute-start.10
  78.8 2.1 collective-permute-start.13
  80.9 3.2 collective-permute-start.12
  84.1 15.7 %collective-permute-done.10.refs_2_ = bf16[112,3584]{1,0:T(8,128)(2,1)} collective-permute-done((bf16[112,3584]{1,0:T(8,128)(2,1)S(1)}, bf16[112,3584]{1,0:T(8,128)(2,1)}, u32[]{:S(2)}, u32[]{:S(2)}) %collective-permute-start.10) | collective-permute-done | bytes 802848 | tf_op jit(solution)/shard_map/ppermute | solution.py:169
  99.8 21.7 %all-to-all-done.1 = bf16[32,8,3584]{2,1,0:T(8,128)(2,1)} async-done(((bf16[32,8,3584]{2,1,0:T(8,128)(2,1)}), bf16[32,8,3584]{2,1,0:T(8,128)(2,1)}, u32[]{:S(2)}, u32[]{:S(2)}) %all-to-all-start.1) | async-done | bytes 1835040 | tf_op jit(solution)/shard_map/all_to_all | solution.py:172
  121.5 1.6 convolution_convert_fusion.2.refs_1_
  123.1 1.1 collective-permute-start.7
  124.2 1.6 convolution_convert_fusion.3.refs_0_
  125.8 1.3 collective-permute-start.4
  127.1 2.2 collective-permute-start.15
  129.3 4.9 %collective-permute-done.14.refs_6_ = bf16[112,3584]{1,0:T(8,128)(2,1)} collective-permute-done((bf16[112,3584]{1,0:T(8,128)(2,1)}, bf16[112,3584]{1,0:T(8,128)(2,1)}, u32[]{:S(2)}, u32[]{:S(2)}) %collective-permute-start.14) | collective-permute-done | bytes 802848 | tf_op jit(solution)/shard_map/ppermute | solution.py:169
  134.2 1.6 collective-permute-start.6
  135.8 8.2 %collective-permute-done.7.refs_5_ = bf16[112,3584]{1,0:T(8,128)(2,1)S(1)} collective-permute-done((bf16[112,3584]{1,0:T(8,128)(2,1)S(1)}, bf16[112,3584]{1,0:T(8,128)(2,1)S(1)}, u32[]{:S(2)}, u32[]{:S(2)}) %collective-permute-start.7) | collective-permute-done | bytes 802848 | tf_op jit(solution)/shard_map/ppermute | solution.py:169
  144.0 2.2 collective-permute-start.9
  146.2 5.1 %collective-permute-done.4.refs_2_ = bf16[112,3584]{1,0:T(8,128)(2,1)S(1)} collective-permute-done((bf16[112,3584]{1,0:T(8,128)(2,1)S(1)}, bf16[112,3584]{1,0:T(8,128)(2,1)S(1)}, u32[]{:S(2)}, u32[]{:S(2)}) %collective-permute-start.4) | collective-permute-done | bytes 802848 | tf_op jit(solution)/shard_map/ppermute | solution.py:169
  151.3 9.9 %collective-permute-done.15.refs_7_ = bf16[112,3584]{1,0:T(8,128)(2,1)S(1)} collective-permute-done((bf16[112,3584]{1,0:T(8,128)(2,1)}, bf16[112,3584]{1,0:T(8,128)(2,1)S(1)}, u32[]{:S(2)}, u32[]{:S(2)}) %collective-permute-start.15) | collective-permute-done | bytes 802848 | tf_op jit(solution)/shard_map/ppermute | solution.py:169
  161.2 2.0 copy-done
  163.3 8.0 %gate_up.2.refs_10_ = f32[896,512]{1,0:T(8,128)S(1)} custom-call(bf16[112,3584]{1,0:T(8,128)(2,1)S(1)} %convolution_convert_fusion.5.refs_0_, bf16[112,3584]{1,0:T(8,128)(2,1)S(1)} %convolution_convert_fusion.4.refs_1_, bf16[112,3584]{1,0:T(8,128)(2,1)} %collective-permute-done.10.refs_2_, bf16[112,3584]{1,0:T(8,128)(2,1)} %collective-permute-done.11.refs_3_, ...), custom_call_target="tpu_custom_call" | custom-call | flops 3288334336 | bytes 10092544 | tf_op jit(solution)/shard_map/gate_up/pallas_call | solution.py:56
  171.3 7.2 %collective-permute-done.6.refs_4_ = bf16[112,3584]{1,0:T(8,128)(2,1)S(1)} collective-permute-done((bf16[112,3584]{1,0:T(8,128)(2,1)S(1)}, bf16[112,3584]{1,0:T(8,128)(2,1)S(1)}, u32[]{:S(2)}, u32[]{:S(2)}) %collective-permute-start.6) | collective-permute-done | bytes 802848 | tf_op jit(solution)/shard_map/ppermute | solution.py:169
  178.4 12.7 %collective-permute-done.9.refs_7_ = bf16[112,3584]{1,0:T(8,128)(2,1)S(1)} collective-permute-done((bf16[112,3584]{1,0:T(8,128)(2,1)S(1)}, bf16[112,3584]{1,0:T(8,128)(2,1)S(1)}, u32[]{:S(2)}, u32[]{:S(2)}) %collective-permute-start.9) | collective-permute-done | bytes 802848 | tf_op jit(solution)/shard_map/ppermute | solution.py:169
  191.1 7.3 %gate_up.3.refs_0_ = bf16[896,256]{1,0:T(8,128)(2,1)S(1)} custom-call(bf16[112,3584]{1,0:T(8,128)(2,1)S(1)} %convolution_convert_fusion.3.refs_0_, bf16[112,3584]{1,0:T(8,128)(2,1)S(1)} %convolution_convert_fusion.2.refs_1_, bf16[112,3584]{1,0:T(8,128)(2,1)S(1)} %collective-permute-done.4.refs_2_, bf16[112,3584]{1,0:T(8,128)(2,1)S(1)} %collective-permute-done.5.refs_3_, ...), custom_call_target="tpu_custom_call" | custom-call | flops 3288334336 | bytes 10092544 | tf_op jit(solution)/shard_map/gate_up/pallas_call | solution.py:56
  199.1 2.7 collective-permute-start.17
  202.5 15.1 %collective-permute-done.16.refs_1_ = bf16[896,256]{1,0:T(8,128)(2,1)S(1)} collective-permute-done((bf16[896,256]{1,0:T(8,128)(2,1)S(1)}, bf16[896,256]{1,0:T(8,128)(2,1)S(1)}, u32[]{:S(2)}, u32[]{:S(2)}) %collective-permute-start.16) | collective-permute-done | bytes 458784 | tf_op jit(solution)/shard_map/ppermute | solution.py:169
  217.6 7.6 %down.1 = bf16[1024,1792]{1,0:T(8,128)(2,1)S(1)} custom-call(bf16[896,256]{1,0:T(8,128)(2,1)S(1)} %gate_up.3.refs_0_, bf16[896,256]{1,0:T(8,128)(2,1)S(1)} %collective-permute-done.16.refs_1_, bf16[896,256]{1,0:T(8,128)(2,1)S(1)} %collective-permute-done.17.refs_2_, bf16[896,256]{1,0:T(8,128)(2,1)S(1)} %collective-permute-done.18.refs_3_, ...), custom_call_target="tpu_custom_call" | custom-call | flops 5637144576 | bytes 7340032 | tf_op jit(solution)/shard_map/down/pallas_call | solution.py:101
  225.2 1.8 copy-done.2
  227.1 15.6 %all-to-all-start.2 = ((bf16[128,8,1792]{2,1,0:T(8,128)(2,1)}), bf16[128,8,1792]{2,1,0:T(8,128)(2,1)}, u32[]{:S(2)}, u32[]{:S(2)}) async-start(bf16[128,8,1792]{2,1,0:T(8,128)(2,1)} %bitcast.55), calls=%async_computation.2 | async-start | bytes 7340032 | tf_op jit(solution)/shard_map/all_to_all | solution.py:172
  243.2 0.8 broadcast_select_fusion
  244.0 2.1 select_n.163
  246.1 1.5 copy.24.mixing_ref
  247.6 77.9 %all-to-all-done.2 = bf16[128,8,1792]{2,1,0:T(8,128)(2,1)} async-done(((bf16[128,8,1792]{2,1,0:T(8,128)(2,1)}), bf16[128,8,1792]{2,1,0:T(8,128)(2,1)}, u32[]{:S(2)}, u32[]{:S(2)}) %all-to-all-start.2) | async-done | bytes 3670048 | tf_op jit(solution)/shard_map/all_to_all | solution.py:172
  325.6 6.9 %mix.1 = bf16[64,7168]{1,0:T(8,128)(2,1)} custom-call(bf16[1024,1792]{1,0:T(8,128)(2,1)} %bitcast.16.returned_ref, bf16[512,1024]{1,0:T(8,128)(2,1)S(1)} %copy.24.mixing_ref, bf16[64,7168]{1,0:T(8,128)(2,1)S(1)} %bitcast.54), custom_call_target="tpu_custom_call" | custom-call | tf_op jit(solution)/shard_map/mix/pallas_call | solution.py:136
  (58 shorter events, 4.8 us)
Async XLA Ops:
  0.0 2.7 collective-permute-start
  5.9 58.6 %all-to-all-start = ((bf16[32,8,3584]{2,1,0:T(8,128)(2,1)}), bf16[32,8,3584]{2,1,0:T(8,128)(2,1)}, u32[]{:S(2)}, u32[]{:S(2)}) async-start(bf16[32,8,3584]{2,1,0:T(8,128)(2,1)} %fusion), calls=%async_computation | async-start | bytes 3670016 | tf_op jit(solution)/shard_map/all_to_all | solution.py:172
  19.5 23.5 %collective-permute-start.1 = (bf16[256,1792]{1,0:T(8,128)(2,1)S(1)}, bf16[256,1792]{1,0:T(8,128)(2,1)S(1)}, u32[]{:S(2)}, u32[]{:S(2)}) collective-permute-start(bf16[256,1792]{1,0:T(8,128)(2,1)S(1)} %get-tuple-element.22), channel_id=1, source_target_pairs={{0,1},{1,2},{2,3},{3,0},{4,5},{5,6},{6,7},{7,4},{8,9},{9,10},{10,1... | collective-permute-start | bytes 2752520 | tf_op jit(solution)/shard_map/ppermute | solution.py:169
  21.1 40.6 %collective-permute-start.2 = (bf16[256,1792]{1,0:T(8,128)(2,1)S(1)}, bf16[256,1792]{1,0:T(8,128)(2,1)S(1)}, u32[]{:S(2)}, u32[]{:S(2)}) collective-permute-start(bf16[256,1792]{1,0:T(8,128)(2,1)S(1)} %get-tuple-element.24), channel_id=1, source_target_pairs={{0,3},{1,0},{2,1},{3,2},{4,7},{5,4},{6,5},{7,6},{8,11},{9,8},{10,9... | collective-permute-start | bytes 2752520 | tf_op jit(solution)/shard_map/ppermute | solution.py:169
  22.8 40.7 %collective-permute-start.3 = (bf16[256,1792]{1,0:T(8,128)(2,1)S(1)}, bf16[256,1792]{1,0:T(8,128)(2,1)S(1)}, u32[]{:S(2)}, u32[]{:S(2)}) collective-permute-start(bf16[256,1792]{1,0:T(8,128)(2,1)S(1)} %get-tuple-element.21), channel_id=1, source_target_pairs={{0,2},{1,3},{2,0},{3,1},{4,6},{5,7},{6,4},{7,5},{8,10},{9,11},{10,... | collective-permute-start | bytes 2752520 | tf_op jit(solution)/shard_map/ppermute | solution.py:169
  42.9 0.9 copy-start.3
  61.7 0.9 copy-start.5
  63.5 1.0 copy-start.7
  67.7 53.8 %all-to-all-start.1 = ((bf16[32,8,3584]{2,1,0:T(8,128)(2,1)}), bf16[32,8,3584]{2,1,0:T(8,128)(2,1)}, u32[]{:S(2)}, u32[]{:S(2)}) async-start(bf16[32,8,3584]{2,1,0:T(8,128)(2,1)} %fusion.1), calls=%async_computation.1 | async-start | bytes 3670016 | tf_op jit(solution)/shard_map/all_to_all | solution.py:172
  77.6 22.2 %collective-permute-start.10 = (bf16[112,3584]{1,0:T(8,128)(2,1)S(1)}, bf16[112,3584]{1,0:T(8,128)(2,1)}, u32[]{:S(2)}, u32[]{:S(2)}) collective-permute-start(bf16[112,3584]{1,0:T(8,128)(2,1)S(1)} %convolution_convert_fusion.5.refs_0_), channel_id=1, source_target_pairs={{0,1},{1,2},{2,3},{3,0},{4,5},{5,6},{6,7},{7,4},{8,9},{9,10},{10,1... | collective-permute-start | bytes 2408456 | tf_op jit(solution)/shard_map/ppermute | solution.py:169
  78.8 47.0 %collective-permute-start.13 = (bf16[112,3584]{1,0:T(8,128)(2,1)S(1)}, bf16[112,3584]{1,0:T(8,128)(2,1)}, u32[]{:S(2)}, u32[]{:S(2)}) collective-permute-start(bf16[112,3584]{1,0:T(8,128)(2,1)S(1)} %convolution_convert_fusion.4.refs_1_), channel_id=1, source_target_pairs={{0,3},{1,0},{2,1},{3,2},{4,7},{5,4},{6,5},{7,6},{8,11},{9,8},{10,9... | collective-permute-start | bytes 2408456 | tf_op jit(solution)/shard_map/ppermute | solution.py:169
  80.9 46.2 %collective-permute-start.11 = (bf16[112,3584]{1,0:T(8,128)(2,1)S(1)}, bf16[112,3584]{1,0:T(8,128)(2,1)}, u32[]{:S(2)}, u32[]{:S(2)}) collective-permute-start(bf16[112,3584]{1,0:T(8,128)(2,1)S(1)} %convolution_convert_fusion.4.refs_1_), channel_id=1, source_target_pairs={{0,1},{1,2},{2,3},{3,0},{4,5},{5,6},{6,7},{7,4},{8,9},{9,10},{10,1... | collective-permute-start | bytes 2408456 | tf_op jit(solution)/shard_map/ppermute | solution.py:169
  80.9 48.4 %collective-permute-start.12 = (bf16[112,3584]{1,0:T(8,128)(2,1)S(1)}, bf16[112,3584]{1,0:T(8,128)(2,1)}, u32[]{:S(2)}, u32[]{:S(2)}) collective-permute-start(bf16[112,3584]{1,0:T(8,128)(2,1)S(1)} %convolution_convert_fusion.5.refs_0_), channel_id=1, source_target_pairs={{0,3},{1,0},{2,1},{3,2},{4,7},{5,4},{6,5},{7,6},{8,11},{9,8},{10,9... | collective-permute-start | bytes 2408456 | tf_op jit(solution)/shard_map/ppermute | solution.py:169
  99.8 34.4 %collective-permute-start.14 = (bf16[112,3584]{1,0:T(8,128)(2,1)}, bf16[112,3584]{1,0:T(8,128)(2,1)}, u32[]{:S(2)}, u32[]{:S(2)}) collective-permute-start(bf16[112,3584]{1,0:T(8,128)(2,1)} %collective-permute-done.10.refs_2_), channel_id=1, source_target_pairs={{0,1},{1,2},{2,3},{3,0},{4,5},{5,6},{6,7},{7,4},{8,9},{9,10},{10,1... | collective-permute-start | bytes 2408456 | tf_op jit(solution)/shard_map/ppermute | solution.py:169
  123.1 20.9 %collective-permute-start.7 = (bf16[112,3584]{1,0:T(8,128)(2,1)S(1)}, bf16[112,3584]{1,0:T(8,128)(2,1)S(1)}, u32[]{:S(2)}, u32[]{:S(2)}) collective-permute-start(bf16[112,3584]{1,0:T(8,128)(2,1)S(1)} %convolution_convert_fusion.2.refs_1_), channel_id=1, source_target_pairs={{0,3},{1,0},{2,1},{3,2},{4,7},{5,4},{6,5},{7,6},{8,11},{9,8},{10,9... | collective-permute-start | bytes 2408456 | tf_op jit(solution)/shard_map/ppermute | solution.py:169
  125.8 25.5 %collective-permute-start.4 = (bf16[112,3584]{1,0:T(8,128)(2,1)S(1)}, bf16[112,3584]{1,0:T(8,128)(2,1)S(1)}, u32[]{:S(2)}, u32[]{:S(2)}) collective-permute-start(bf16[112,3584]{1,0:T(8,128)(2,1)S(1)} %convolution_convert_fusion.3.refs_0_), channel_id=1, source_target_pairs={{0,1},{1,2},{2,3},{3,0},{4,5},{5,6},{6,7},{7,4},{8,9},{9,10},{10,1... | collective-permute-start | bytes 2408456 | tf_op jit(solution)/shard_map/ppermute | solution.py:169
  127.1 34.1 %collective-permute-start.15 = (bf16[112,3584]{1,0:T(8,128)(2,1)}, bf16[112,3584]{1,0:T(8,128)(2,1)S(1)}, u32[]{:S(2)}, u32[]{:S(2)}) collective-permute-start(bf16[112,3584]{1,0:T(8,128)(2,1)} %collective-permute-done.13.refs_5_), channel_id=1, source_target_pairs={{0,3},{1,0},{2,1},{3,2},{4,7},{5,4},{6,5},{7,6},{8,11},{9,8},{10,9... | collective-permute-start | bytes 2408456 | tf_op jit(solution)/shard_map/ppermute | solution.py:169
  129.3 42.0 %collective-permute-start.5 = (bf16[112,3584]{1,0:T(8,128)(2,1)S(1)}, bf16[112,3584]{1,0:T(8,128)(2,1)S(1)}, u32[]{:S(2)}, u32[]{:S(2)}) collective-permute-start(bf16[112,3584]{1,0:T(8,128)(2,1)S(1)} %convolution_convert_fusion.2.refs_1_), channel_id=1, source_target_pairs={{0,1},{1,2},{2,3},{3,0},{4,5},{5,6},{6,7},{7,4},{8,9},{9,10},{10,1... | collective-permute-start | bytes 2408456 | tf_op jit(solution)/shard_map/ppermute | solution.py:169
  134.2 44.2 %collective-permute-start.6 = (bf16[112,3584]{1,0:T(8,128)(2,1)S(1)}, bf16[112,3584]{1,0:T(8,128)(2,1)S(1)}, u32[]{:S(2)}, u32[]{:S(2)}) collective-permute-start(bf16[112,3584]{1,0:T(8,128)(2,1)S(1)} %convolution_convert_fusion.3.refs_0_), channel_id=1, source_target_pairs={{0,3},{1,0},{2,1},{3,2},{4,7},{5,4},{6,5},{7,6},{8,11},{9,8},{10,9... | collective-permute-start | bytes 2408456 | tf_op jit(solution)/shard_map/ppermute | solution.py:169
  144.0 47.1 %collective-permute-start.9 = (bf16[112,3584]{1,0:T(8,128)(2,1)S(1)}, bf16[112,3584]{1,0:T(8,128)(2,1)S(1)}, u32[]{:S(2)}, u32[]{:S(2)}) collective-permute-start(bf16[112,3584]{1,0:T(8,128)(2,1)S(1)} %collective-permute-done.7.refs_5_), channel_id=1, source_target_pairs={{0,3},{1,0},{2,1},{3,2},{4,7},{5,4},{6,5},{7,6},{8,11},{9,8},{10,9... | collective-permute-start | bytes 2408456 | tf_op jit(solution)/shard_map/ppermute | solution.py:169
  151.3 39.8 %collective-permute-start.8 = (bf16[112,3584]{1,0:T(8,128)(2,1)S(1)}, bf16[112,3584]{1,0:T(8,128)(2,1)S(1)}, u32[]{:S(2)}, u32[]{:S(2)}) collective-permute-start(bf16[112,3584]{1,0:T(8,128)(2,1)S(1)} %collective-permute-done.4.refs_2_), channel_id=1, source_target_pairs={{0,1},{1,2},{2,3},{3,0},{4,5},{5,6},{6,7},{7,4},{8,9},{9,10},{10,1... | collective-permute-start | bytes 2408456 | tf_op jit(solution)/shard_map/ppermute | solution.py:169
  161.2 2.0 copy-start
  163.3 27.8 %copy-start.1 = (bf16[1,7168,256]{2,1,0:T(8,128)(2,1)S(1)}, bf16[1,7168,256]{2,1,0:T(8,128)(2,1)}, u32[]{:S(2)}) copy-start(bf16[1,7168,256]{2,1,0:T(8,128)(2,1)} %param.11) | copy-start | bytes 11010052
  191.1 26.5 %copy-start.8 = (bf16[256,1792]{1,0:T(8,128)(2,1)S(1)}, bf16[256,1792]{1,0:T(8,128)(2,1)}, u32[]{:S(2)}) copy-start(bf16[256,1792]{1,0:T(8,128)(2,1)} %copy-done.7) | copy-start | bytes 2752516
  198.4 19.2 %copy-start.4 = (bf16[256,1792]{1,0:T(8,128)(2,1)S(1)}, bf16[256,1792]{1,0:T(8,128)(2,1)}, u32[]{:S(2)}) copy-start(bf16[256,1792]{1,0:T(8,128)(2,1)} %copy-done.3) | copy-start | bytes 2752516
  198.4 19.2 %copy-start.6 = (bf16[256,1792]{1,0:T(8,128)(2,1)S(1)}, bf16[256,1792]{1,0:T(8,128)(2,1)}, u32[]{:S(2)}) copy-start(bf16[256,1792]{1,0:T(8,128)(2,1)} %copy-done.5) | copy-start | bytes 2752516
  198.4 19.1 %collective-permute-start.16 = (bf16[896,256]{1,0:T(8,128)(2,1)S(1)}, bf16[896,256]{1,0:T(8,128)(2,1)S(1)}, u32[]{:S(2)}, u32[]{:S(2)}) collective-permute-start(bf16[896,256]{1,0:T(8,128)(2,1)S(1)} %gate_up.3.refs_0_), channel_id=1, source_target_pairs={{0,1},{1,2},{2,3},{3,0},{4,5},{5,6},{6,7},{7,4},{8,9},{9,10},{10,1... | collective-permute-start | bytes 1376264 | tf_op jit(solution)/shard_map/ppermute | solution.py:169
  199.1 18.5 %collective-permute-start.17 = (bf16[896,256]{1,0:T(8,128)(2,1)S(1)}, bf16[896,256]{1,0:T(8,128)(2,1)S(1)}, u32[]{:S(2)}, u32[]{:S(2)}) collective-permute-start(bf16[896,256]{1,0:T(8,128)(2,1)S(1)} %gate_up.3.refs_0_), channel_id=1, source_target_pairs={{0,3},{1,0},{2,1},{3,2},{4,7},{5,4},{6,5},{7,6},{8,11},{9,8},{10,9... | collective-permute-start | bytes 1376264 | tf_op jit(solution)/shard_map/ppermute | solution.py:169
  201.8 15.8 %collective-permute-start.18 = (bf16[896,256]{1,0:T(8,128)(2,1)S(1)}, bf16[896,256]{1,0:T(8,128)(2,1)S(1)}, u32[]{:S(2)}, u32[]{:S(2)}) collective-permute-start(bf16[896,256]{1,0:T(8,128)(2,1)S(1)} %gate_up.3.refs_0_), channel_id=1, source_target_pairs={{0,2},{1,3},{2,0},{3,1},{4,6},{5,7},{6,4},{7,5},{8,10},{9,11},{10,... | collective-permute-start | bytes 1376264 | tf_op jit(solution)/shard_map/ppermute | solution.py:169
  225.2 1.8 copy-start.2
  227.1 15.6 %copy-start.9 = (f32[1,64,3]{1,0,2:T(1,128)S(1)}, f32[1,64,3]{1,0,2:T(1,128)}, u32[]{:S(2)}) copy-start(f32[1,64,3]{1,0,2:T(1,128)} %param.10) | copy-start | bytes 2308
  227.1 98.5 %all-to-all-start.2 = ((bf16[128,8,1792]{2,1,0:T(8,128)(2,1)}), bf16[128,8,1792]{2,1,0:T(8,128)(2,1)}, u32[]{:S(2)}, u32[]{:S(2)}) async-start(bf16[128,8,1792]{2,1,0:T(8,128)(2,1)} %bitcast.55), calls=%async_computation.2 | async-start | bytes 7340032 | tf_op jit(solution)/shard_map/all_to_all | solution.py:172
where the time goes:
time: 333 us; the launch traced here: 332 us
  waiting for transfers between devices  214 us (64%)
  starting transfers between devices  60.2 us (18%)
  Pallas kernels  29.8 us (9%)
  local copies, waits for them, and re-layouts  14.1 us (4%)
  matrix products  10.2 us (3%)
  other arithmetic  3.97 us (1%)
    ppermute x18, waiting for transfers between devices, shift(): return lax.ppermute(block, 'expert', route)  114 us
    all_to_all x3, waiting for transfers between devices, exchange(): lax.all_to_all(block, 'expert', split_axis=0, concat_axis=0, axis_index_g...  99.7 us
    all_to_all x3, starting transfers between devices, exchange(): lax.all_to_all(block, 'expert', split_axis=0, concat_axis=0, axis_index_g...  36.7 us
    ppermute x18, starting transfers between devices, shift(): return lax.ppermute(block, 'expert', route)  23.5 us
    pallas_call x2, Pallas kernels, gate_up(): pl.pallas_call(functools.partial(gate_up_kernel, len(pieces), steps, last...  15.3 us
    pallas_call x1, Pallas kernels, down(): pl.pallas_call(functools.partial(down_kernel, orders), grid=(width // col...  7.62 us
    unnamed x22, local copies, waits for them, and re-layouts  7.5 us
    pallas_call x1, Pallas kernels, mix(): pl.pallas_call(functools.partial(mix_kernel, parts, width), grid=(width /...  6.89 us
  transfers between devices with their start and end apart: 22, of which 14 were waited for; matrix products, arithmetic and copies ran while one was open for 5% of the time, Pallas kernels for 2%

commit v1 on v0

--- a/solution.py
+++ b/solution.py
@@ -9,10 +9,37 @@
 
 FF_WIN = 1024
 HID_DEV = 256
-CHUNKS = 2
+WIDTHS = (4096, 3072)
+FOLD = 8
 PAD = 8
+VMEM = 40 << 20
 
 epsilon = 1e-06
+
+
+def unfold_kernel(sort_ref, landed_ref, *out_refs):
+    cols = landed_ref.shape[1]
+    rows = landed_ref.shape[0] // len(out_refs)
+    for h, out_ref in enumerate(out_refs):
+        count = out_ref.shape[0]
+        part = landed_ref[h * rows : (h + 1) * rows, :]
+        sorted_part = jnp.dot(sort_ref[...], part, preferred_element_type=jnp.float32)
+        sorted_part = sorted_part.astype(out_ref.dtype)
+        for f in range(FOLD):
+            out_ref[:, f * cols : (f + 1) * cols] = sorted_part[f * count : (f + 1) * count]
+
+
+def unfold(landed, sort):
+    rows, cols = landed.shape
+    count = sort.shape[0] // FOLD
+    halves = rows // sort.shape[0]
+    shape = jax.ShapeDtypeStruct((count, cols * FOLD), landed.dtype)
+    return pl.pallas_call(
+        unfold_kernel,
+        out_shape=[shape] * halves,
+        compiler_params=pltpu.CompilerParams(vmem_limit_bytes=VMEM),
+        name="unfold",
+    )(sort, landed)
 
 
 def gate_up_kernel(pieces, steps, last, *refs):
@@ -43,9 +70,9 @@
             out_ref[...] = acc_ref[...]
 
 
-def gate_up(pieces, gate_weight, up_weight, first_row, before, last):
+def gate_up(pieces, gate_weight, up_weight, first_row, before, block, last):
     piece_rows, width = pieces[0].shape
-    depth = 512
+    depth = 1024
     steps = width // depth
     offset = first_row // depth
     rows = piece_rows * len(pieces)
@@ -58,11 +85,11 @@
         grid=(steps,),
         in_specs=[pl.BlockSpec((piece_rows, depth), lambda k: (0, k)) for _ in pieces]
         + [pl.BlockSpec((depth, hid), lambda k: (k + offset, 0))] * 2
-        + [pl.BlockSpec((rows, 2 * hid), lambda k: (0, 0)) for _ in start],
+        + [pl.BlockSpec((rows, 2 * hid), lambda k: (block, 0)) for _ in start],
         out_specs=pl.BlockSpec(out_shape, lambda k: (0, 0)),
         out_shape=jax.ShapeDtypeStruct(out_shape, out_type),
         scratch_shapes=[pltpu.VMEM((rows, 2 * hid), jnp.float32)],
-        compiler_params=pltpu.CompilerParams(vmem_limit_bytes=40 << 20),
+        compiler_params=pltpu.CompilerParams(vmem_limit_bytes=VMEM),
         cost_estimate=pl.CostEstimate(
             flops=4 * rows * hid * width, bytes_accessed=2 * (rows + 2 * hid) * width, transcendentals=0
         ),
@@ -72,17 +99,17 @@
 
 def down_kernel(orders, *refs):
     parts = len(orders)
-    hid_refs, weight_refs = refs[:parts], refs[parts : 2 * parts]
-    spread_ref, out_ref, spread_hid = refs[2 * parts :]
-    hid = hid_refs[0].shape[1]
-    block = hid_refs[0].shape[0] // parts
+    near_refs, far_refs = refs[:parts], refs[parts : 2 * parts]
+    weight_refs = refs[2 * parts : 3 * parts]
+    spread_ref, out_ref, spread_hid = refs[3 * parts :]
+    block, hid = far_refs[0].shape
 
     @pl.when(pl.program_id(0) == 0)
     def _():
         for j in range(parts):
-            rows = jnp.concatenate(
-                [hid_refs[j][b * block : (b + 1) * block, :] for b in orders[j]], axis=0
-            )
+            blocks = [near_refs[j][b * block : (b + 1) * block, :] for b in range(parts - 1)]
+            blocks.append(far_refs[j][...])
+            rows = jnp.concatenate([blocks[b] for b in orders[j]], axis=0)
             spread_hid[:, j * hid : (j + 1) * hid] = jnp.dot(
                 spread_ref[...], rows, preferred_element_type=jnp.float32
             ).astype(spread_hid.dtype)
@@ -93,28 +120,29 @@
     )
 
 
-def down(hiddens, weights, spread, orders):
-    rows, hid = hiddens[0].shape
+def down(near, far, weights, spread, orders):
+    hid = far[0].shape[1]
     out_rows, width = spread.shape[0], weights[0].shape[1]
-    cols = 896
+    cols = width // 2
     parts = len(orders)
     return pl.pallas_call(
         functools.partial(down_kernel, orders),
         grid=(width // cols,),
-        in_specs=[pl.BlockSpec((rows, hid), lambda n: (0, 0))] * parts
+        in_specs=[pl.BlockSpec(near[0].shape, lambda n: (0, 0))] * parts
+        + [pl.BlockSpec(far[0].shape, lambda n: (0, 0))] * parts
         + [pl.BlockSpec((hid, cols), lambda n: (0, n))] * parts
         + [pl.BlockSpec(spread.shape, lambda n: (0, 0))],
         out_specs=pl.BlockSpec((out_rows, cols), lambda n: (0, n)),
         out_shape=jax.ShapeDtypeStruct((out_rows, width), jnp.bfloat16),
         scratch_shapes=[pltpu.VMEM((out_rows, parts * hid), jnp.bfloat16)],
-        compiler_params=pltpu.CompilerParams(vmem_limit_bytes=40 << 20),
+        compiler_params=pltpu.CompilerParams(vmem_limit_bytes=VMEM),
         cost_estimate=pl.CostEstimate(
-            flops=2 * out_rows * parts * hid * (width + rows),
+            flops=2 * out_rows * parts * hid * (width + spread.shape[1]),
             bytes_accessed=2 * (out_rows + parts * hid) * width,
             transcendentals=0,
         ),
         name="down",
-    )(*hiddens, *weights, spread)
+    )(*near, *far, *weights, spread)
 
 
 def mix_kernel(parts, width, returned_ref, mixing_ref, inbound_ref, out_ref):
@@ -132,7 +160,7 @@
 
 def mix(returned, mixing, inbound, parts):
     rows, width = returned.shape
-    cols = 256
+    cols = 896
     return pl.pallas_call(
         functools.partial(mix_kernel, parts, width),
         grid=(width // cols,),
@@ -143,7 +171,7 @@
         ],
         out_specs=pl.BlockSpec(inbound.shape, lambda n: (0, 0)),
         out_shape=jax.ShapeDtypeStruct(inbound.shape, inbound.dtype),
-        compiler_params=pltpu.CompilerParams(vmem_limit_bytes=40 << 20),
+        compiler_params=pltpu.CompilerParams(vmem_limit_bytes=VMEM),
         name="mix",
     )(returned, mixing, inbound)
 
@@ -157,9 +185,7 @@
     top_count = routes.shape[2]
     capacity = min(tok_count, 5 * tok_count * top_count // (4 * experts))
     slots = experts * capacity
-    padded = experts * PAD
     half = slots // 2
-    width = feature_count // CHUNKS
     quarter = feature_count // ring
     planes = [[g * ring + r for g in range(experts)] for r in range(ring)]
     place = lax.rem(lax.axis_index("expert"), ring)
@@ -176,6 +202,9 @@
     def weight_part(step):
         start = lax.rem(place + step, ring) * quarter
         return lax.dynamic_slice_in_dim(down_weight[0], start, quarter, 1)
+
+    def numbers(count):
+        return jnp.arange(count, dtype=jnp.int32)
 
     other = [(i, 1 - i) for i in range(2)]
     inbound = lax.ppermute(arriving, "section", other)[0]
@@ -193,46 +222,50 @@
     earlier = jnp.cumsum(onehot, axis=0) - onehot
     slot_index = jnp.sum(earlier * onehot, axis=1)
     target = (chosen * PAD + slot_index).reshape(tok_count, top_count)
-    slot_ids = jnp.arange(padded, dtype=jnp.int32)
-    hits = target[:, :, None] == slot_ids[None, None, :]
-    placement = jnp.any(hits, axis=1).astype(jnp.bfloat16).T
-
-    def rows_of(count, size):
-        ids = jnp.arange(count * size, dtype=jnp.int32)
-        return ids // size, ids % size
-
-    to_block, to_slot = rows_of(experts // 2, capacity)
-    from_block, from_slot = rows_of(experts // 2, PAD)
-    squeeze = (to_block * PAD + to_slot)[:, None] == (from_block * PAD + from_slot)[None, :]
-    squeeze = squeeze.astype(jnp.bfloat16)
-
-    def squeezed(block):
-        return jnp.dot(squeeze, block, preferred_element_type=jnp.float32).astype(jnp.bfloat16)
-
-    packed = [
-        jnp.dot(placement, normed[:, c * width : (c + 1) * width], preferred_element_type=jnp.float32)
-        .astype(jnp.bfloat16)
-        .reshape(experts, PAD, width)
-        for c in range(CHUNKS)
-    ]
-    state = None
-    for c in range(CHUNKS):
-        landed = exchange(packed[c], planes).reshape(padded, width)
-        if c == 0:
-            landed, *down_parts = lax.optimization_barrier((landed, *down_parts))
-        first, second = squeezed(landed[: padded // 2]), squeezed(landed[padded // 2 :])
-        if c + 1 < CHUNKS:
-            first, second, packed[c + 1] = lax.optimization_barrier((first, second, packed[c + 1]))
+
+    row, token = numbers(experts * FOLD * capacity), numbers(FOLD * tok_count)
+    code = row // (FOLD * capacity) * PAD + row % capacity
+    hits = jnp.any(jnp.tile(target, (FOLD, 1))[None, :, :] == code[:, None, None], axis=2)
+    hits = hits & ((row % (FOLD * capacity) // capacity)[:, None] == (token // tok_count)[None, :])
+    placement = hits.astype(jnp.bfloat16)
+    packed, firsts = [], []
+    for width in WIDTHS:
+        firsts.append(firsts[-1] + WIDTHS[len(firsts) - 1] if firsts else 0)
+        cols = width // FOLD
+        cuts = [firsts[-1] + f * cols for f in range(FOLD)]
+        folded = jnp.concatenate([normed[:, cut : cut + cols] for cut in cuts], axis=0)
+        block = jnp.dot(placement, folded, preferred_element_type=jnp.float32)
+        packed.append(block.astype(jnp.bfloat16).reshape(experts, FOLD * capacity, cols))
+
+    to_row, from_row = numbers(FOLD * half), numbers(FOLD * half)
+    wanted = to_row % half // capacity * (FOLD * capacity) + to_row // half * capacity + to_row % capacity
+    sort = (wanted[:, None] == from_row[None, :]).astype(jnp.bfloat16)
+
+    gate, up = gate_weight[0], up_weight[0]
+    packed[1], *down_parts = lax.optimization_barrier((packed[1], *down_parts))
+    landed = [exchange(block, planes) for block in packed]
+    landed = [block.reshape(FOLD * slots, block.shape[2]) for block in landed]
+    arrived = []
+    for c in range(len(WIDTHS)):
+        if c > 0:
+            early = arrived[c - 1][2], arrived[c - 1][5]
+            landed[c] = lax.optimization_barrier((landed[c], *early))[0]
+        first, second = unfold(landed[c], sort)
         left_first, right_second = shift(first, 1), shift(second, -1)
         left_second, right_first = shift(second, 1), shift(first, -1)
         far_first, far_second = shift(left_first, 1), shift(right_second, -1)
-        pieces = [
-            first, second, left_first, left_second, right_first, right_second, far_first, far_second
-        ]
-        state = gate_up(
-            pieces, gate_weight[0], up_weight[0], c * width, state, c == CHUNKS - 1
+        arrived.append(
+            [first, second, left_first, left_second, right_first, right_second, far_first, far_second]
         )
-    hiddens = [state, shift(state, 1), shift(state, -1), shift(state, 2)]
+    state = None
+    for c in range(len(WIDTHS) - 1):
+        early = arrived[c + 1][2], arrived[c + 1][5]
+        begun = list(lax.optimization_barrier((*arrived[c], *early))[: len(arrived[c])])
+        state = gate_up(begun, gate, up, firsts[c], state, 0, False)
+    mine_near = gate_up(arrived[-1][:6], gate, up, firsts[-1], state, 0, True)
+    near = [mine_near, shift(mine_near, 1), shift(mine_near, -1), shift(mine_near, 2)]
+    mine_far = gate_up(arrived[-1][6:], gate, up, firsts[-1], state, 3, True)
+    far = [mine_far, shift(mine_far, 1), shift(mine_far, -1), shift(mine_far, 2)]
     orders = ((0, 1, 2, 3), (2, 0, 3, 1), (1, 3, 0, 2), (3, 2, 1, 0))
 
     row = jnp.arange(device_count * PAD, dtype=jnp.int32)
@@ -243,10 +276,11 @@
     inner = column % slots
     goal = (inner // capacity * ring + origin) * PAD + inner % capacity
     spread = (row[:, None] == goal[None, :]).astype(jnp.bfloat16)
-    complete = down(hiddens, down_parts, spread, orders)
+    complete = down(near, far, down_parts, spread, orders)
     returned = exchange(complete.reshape(device_count, PAD, quarter), None)
     returned = returned.reshape(device_count * PAD, quarter)
 
+    hits = target[:, :, None] == numbers(experts * PAD)[None, None, :]
     mixing = jnp.sum(jnp.where(hits, combine_weight[0][:, :, None], 0.0), axis=1)
     mix_high = lax.reduce_precision(mixing, 8, 7)
     both = jnp.stack([mix_high, mixing - mix_high]).astype(jnp.bfloat16)

time: 333 us -> 317 us (0.952)
  waiting for transfers between devices: 214 us -> 191 us
  Pallas kernels: 29.8 us -> 36.4 us
  matrix products: 10.2 us -> 5.18 us
  starting transfers between devices: 60.2 us -> 64.2 us
    ppermute x18 -> x21, waiting for transfers between devices: 114 us -> 92.5 us  [shift(): return lax.ppermute(block, 'expert', route)]
    pallas_call x0 -> x2, Pallas kernels: none -> 8.89 us  [unfold(): pl.pallas_call(unfold_kernel, out_shape=[shape] * halves, compiler_params...]
    ppermute x18 -> x21, starting transfers between devices: 23.5 us -> 31.6 us  [shift(): return lax.ppermute(block, 'expert', route)]
    dot_general x6 -> x2, matrix products: 10.2 us -> 5.18 us  [body(): block = jnp.dot(placement, folded, preferred_element_type=jnp.float32)]
    all_to_all x3, starting transfers between devices: 36.7 us -> 32.6 us  [exchange(): lax.all_to_all(block, 'expert', split_axis=0, concat_axis=0, axis_index_g...]
    pallas_call x2 -> x3, Pallas kernels: 15.3 us -> 14.9 us  [gate_up(): pl.pallas_call(functools.partial(gate_up_kernel, len(pieces), steps, last...]
    unnamed x22 -> x44, local copies, waits for them, and re-layouts: 7.5 us -> 7.67 us
  transfers between devices with their start and end apart: 22 -> 25, of which waited for: 14 -> 13; matrix products, arithmetic and copies ran while one was open for 5% -> 4% of each run, Pallas kernels for 2% -> 8%
where the time goes in v1:
time: 317 us; the launch traced here: 316 us
  waiting for transfers between devices  191 us (60%)
  starting transfers between devices  64.2 us (20%)
  Pallas kernels  36.4 us (11%)
  local copies, waits for them, and re-layouts  14.5 us (5%)
  matrix products  5.18 us (2%)
  other arithmetic  4.5 us (1%)
    all_to_all x3, waiting for transfers between devices, exchange(): lax.all_to_all(block, 'expert', split_axis=0, concat_axis=0, axis_index_g...  98.8 us
    ppermute x21, waiting for transfers between devices, shift(): return lax.ppermute(block, 'expert', route)  92.5 us
    all_to_all x3, starting transfers between devices, exchange(): lax.all_to_all(block, 'expert', split_axis=0, concat_axis=0, axis_index_g...  32.6 us
    ppermute x21, starting transfers between devices, shift(): return lax.ppermute(block, 'expert', route)  31.6 us
    pallas_call x3, Pallas kernels, gate_up(): pl.pallas_call(functools.partial(gate_up_kernel, len(pieces), steps, last...  14.9 us
    pallas_call x2, Pallas kernels, unfold(): pl.pallas_call(unfold_kernel, out_shape=[shape] * halves, compiler_params...  8.89 us
    unnamed x44, local copies, waits for them, and re-layouts  7.67 us
    pallas_call x1, Pallas kernels, down(): pl.pallas_call(functools.partial(down_kernel, orders), grid=(width // col...  7.63 us
  transfers between devices with their start and end apart: 25, of which 13 were waited for; matrix products, arithmetic and copies ran while one was open for 4% of the time, Pallas kernels for 8%

profile of v1, /device:TPU:32, one launch (start us, length us, event | category | flops | bytes accessed | tf_op | source)
XLA Modules:
  0.0 316.5 jit_solution(539144472103590388)
XLA Ops:
  2.3 1.0 compare_reduce_fusion
  4.0 2.7 convolution_convert_fusion
  6.7 11.2 %all-to-all-start.1 = ((bf16[32,56,512]{2,1,0:T(8,128)(2,1)}), bf16[32,56,512]{2,1,0:T(8,128)(2,1)}, u32[]{:S(2)}, u32[]{:S(2)}) async-start(bf16[32,56,512]{2,1,0:T(8,128)(2,1)} %bitcast.55), calls=%async_computation.1 | async-start | bytes 3670016 | tf_op jit(solution)/shard_map/all_to_all | solution.py:198
  18.0 2.3 dynamic-slice_bitcast_fusion
  20.3 1.7 collective-permute-start.1
  22.0 1.7 collective-permute-start.2
  23.6 2.0 collective-permute-start.3
  25.7 2.5 convolution_convert_fusion.1
  28.3 15.6 %collective-permute-done.1.refs_9_ = bf16[256,1792]{1,0:T(8,128)(2,1)S(1)} collective-permute-done((bf16[256,1792]{1,0:T(8,128)(2,1)S(1)}, bf16[256,1792]{1,0:T(8,128)(2,1)S(1)}, u32[]{:S(2)}, u32[]{:S(2)}) %collective-permute-start.1) | collective-permute-done | bytes 917536 | tf_op jit(solution)/shard_map/ppermute | solution.py:195
  43.9 0.9 copy-done.4
  44.8 18.1 %collective-permute-done.2.refs_10_ = bf16[256,1792]{1,0:T(8,128)(2,1)S(1)} collective-permute-done((bf16[256,1792]{1,0:T(8,128)(2,1)S(1)}, bf16[256,1792]{1,0:T(8,128)(2,1)S(1)}, u32[]{:S(2)}, u32[]{:S(2)}) %collective-permute-start.2) | collective-permute-done | bytes 917536 | tf_op jit(solution)/shard_map/ppermute | solution.py:195
  62.9 1.0 copy-done.6
  64.7 0.9 copy-done.8
  65.6 9.8 %all-to-all-start = ((bf16[32,56,384]{2,1,0:T(8,128)(2,1)}), bf16[32,56,384]{2,1,0:T(8,128)(2,1)}, u32[]{:S(2)}, u32[]{:S(2)}) async-start(bf16[32,56,384]{2,1,0:T(8,128)(2,1)} %bitcast.4), calls=%async_computation | async-start | bytes 2752512 | tf_op jit(solution)/shard_map/all_to_all | solution.py:198
  75.8 4.7 %unfold.2 = (bf16[112,4096]{1,0:T(8,128)(2,1)}, bf16[112,4096]{1,0:T(8,128)(2,1)}) custom-call(bf16[896,896]{1,0:T(8,128)(2,1)S(1)} %fusion.1.sort_ref, bf16[1792,512]{1,0:T(8,128)(2,1)} %bitcast.11.landed_ref), custom_call_target="tpu_custom_call" | custom-call | tf_op jit(solution)/shard_map/unfold/pallas_call | solution.py:37
  80.5 1.1 collective-permute-start.4
  81.6 2.1 collective-permute-start.5
  83.7 3.2 %collective-permute-start.11 = (bf16[112,4096]{1,0:T(8,128)(2,1)}, bf16[112,4096]{1,0:T(8,128)(2,1)}, u32[]{:S(2)}, u32[]{:S(2)}) collective-permute-start(bf16[112,4096]{1,0:T(8,128)(2,1)} %get-tuple-element.29.refs_0_), channel_id=1, source_target_pairs={{0,3},{1,0},{2,1},{3,2},{4,7},{5,4},{6,5},{7,6},{8,11},{9,8},{10,9... | collective-permute-start | bytes 2752520 | tf_op jit(solution)/shard_map/ppermute | solution.py:195
  87.0 22.9 %all-to-all-done = bf16[32,56,384]{2,1,0:T(8,128)(2,1)} async-done(((bf16[32,56,384]{2,1,0:T(8,128)(2,1)}), bf16[32,56,384]{2,1,0:T(8,128)(2,1)}, u32[]{:S(2)}, u32[]{:S(2)}) %all-to-all-start) | async-done | bytes 1376288 | tf_op jit(solution)/shard_map/all_to_all | solution.py:198
  109.9 4.2 %unfold.3 = (bf16[112,3072]{1,0:T(8,128)(2,1)}, bf16[112,3072]{1,0:T(8,128)(2,1)}) custom-call(bf16[896,896]{1,0:T(8,128)(2,1)S(1)} %fusion.1.sort_ref, bf16[1792,384]{1,0:T(8,128)(2,1)} %bitcast.9.landed_ref), custom_call_target="tpu_custom_call" | custom-call | tf_op jit(solution)/shard_map/unfold/pallas_call | solution.py:37
  115.2 2.9 collective-permute-start.13
  118.1 6.8 %collective-permute-done.10.refs_3_ = bf16[112,4096]{1,0:T(8,128)(2,1)} collective-permute-done((bf16[112,4096]{1,0:T(8,128)(2,1)}, bf16[112,4096]{1,0:T(8,128)(2,1)}, u32[]{:S(2)}, u32[]{:S(2)}) %collective-permute-start.10) | collective-permute-done | bytes 917536 | tf_op jit(solution)/shard_map/ppermute | solution.py:195
  125.0 1.6 collective-permute-start.9
  127.0 12.6 %collective-permute-done.6.refs_2_ = bf16[112,3072]{1,0:T(8,128)(2,1)S(1)} collective-permute-done((bf16[112,3072]{1,0:T(8,128)(2,1)}, bf16[112,3072]{1,0:T(8,128)(2,1)S(1)}, u32[]{:S(2)}, u32[]{:S(2)}) %collective-permute-start.6) | collective-permute-done | bytes 688160 | tf_op jit(solution)/shard_map/ppermute | solution.py:195
  139.6 1.6 collective-permute-start.8
  141.2 18.0 %collective-permute-done.9.refs_5_ = bf16[112,3072]{1,0:T(8,128)(2,1)S(1)} collective-permute-done((bf16[112,3072]{1,0:T(8,128)(2,1)}, bf16[112,3072]{1,0:T(8,128)(2,1)S(1)}, u32[]{:S(2)}, u32[]{:S(2)}) %collective-permute-start.9) | collective-permute-done | bytes 688160 | tf_op jit(solution)/shard_map/ppermute | solution.py:195
  159.2 1.5 collective-permute-start.17
  160.7 1.8 collective-permute-start.18
  162.5 2.0 copy-done
  164.6 7.4 %gate_up.3.refs_8_.refs_4_ = f32[896,512]{1,0:T(8,128)S(1)} custom-call(bf16[112,4096]{1,0:T(8,128)(2,1)} %get-tuple-element.29.refs_0_, bf16[112,4096]{1,0:T(8,128)(2,1)} %get-tuple-element.30.refs_1_, bf16[112,4096]{1,0:T(8,128)(2,1)} %collective-permute-done.4.refs_2_, bf16[112,4096]{1,0:T(8,128)(2,1)} %collective-permute-done.10.refs_3_, ...), custom_call_target="tpu_custom_call" | custom-call | flops 3758096384 | bytes 11534336 | tf_op jit(solution)/shard_map/gate_up/pallas_call | solution.py:83
  172.0 2.1 collective-permute-done.7.refs_3_
  174.1 4.6 %gate_up.4.refs_0_ = bf16[672,256]{1,0:T(8,128)(2,1)S(1)} custom-call(bf16[112,3072]{1,0:T(8,128)(2,1)} %get-tuple-element.27.refs_0_, bf16[112,3072]{1,0:T(8,128)(2,1)} %get-tuple-element.28.refs_1_, bf16[112,3072]{1,0:T(8,128)(2,1)S(1)} %collective-permute-done.6.refs_2_, bf16[112,3072]{1,0:T(8,128)(2,1)} %collective-permute-done.7.refs_3_, ...), custom_call_target="tpu_custom_call" | custom-call | flops 2113929216 | bytes 7274496 | tf_op jit(solution)/shard_map/gate_up/pallas_call | solution.py:83
  178.8 1.5 collective-permute-start.14
  180.3 1.9 collective-permute-start.15
  182.2 1.8 collective-permute-start.16
  184.0 4.7 %collective-permute-done.17.refs_0_ = bf16[112,3072]{1,0:T(8,128)(2,1)S(1)} collective-permute-done((bf16[112,3072]{1,0:T(8,128)(2,1)S(1)}, bf16[112,3072]{1,0:T(8,128)(2,1)S(1)}, u32[]{:S(2)}, u32[]{:S(2)}) %collective-permute-start.17) | collective-permute-done | bytes 688160 | tf_op jit(solution)/shard_map/ppermute | solution.py:195
  188.8 2.8 gate_up.5.refs_4_
  191.7 1.1 collective-permute-start.19
  192.8 2.5 collective-permute-start.20
  195.3 8.1 %collective-permute-done.14.refs_1_ = bf16[672,256]{1,0:T(8,128)(2,1)S(1)} collective-permute-done((bf16[672,256]{1,0:T(8,128)(2,1)S(1)}, bf16[672,256]{1,0:T(8,128)(2,1)S(1)}, u32[]{:S(2)}, u32[]{:S(2)}) %collective-permute-start.14) | collective-permute-done | bytes 344096 | tf_op jit(solution)/shard_map/ppermute | solution.py:195
  204.7 5.1 %collective-permute-done.21.refs_7_ = bf16[224,256]{1,0:T(8,128)(2,1)S(1)} collective-permute-done((bf16[224,256]{1,0:T(8,128)(2,1)S(1)}, bf16[224,256]{1,0:T(8,128)(2,1)S(1)}, u32[]{:S(2)}, u32[]{:S(2)}) %collective-permute-start.21) | collective-permute-done | bytes 114720 | tf_op jit(solution)/shard_map/ppermute | solution.py:195
  209.8 7.6 %down.1 = bf16[1024,1792]{1,0:T(8,128)(2,1)S(1)} custom-call(bf16[672,256]{1,0:T(8,128)(2,1)S(1)} %gate_up.4.refs_0_, bf16[672,256]{1,0:T(8,128)(2,1)S(1)} %collective-permute-done.14.refs_1_, bf16[672,256]{1,0:T(8,128)(2,1)S(1)} %collective-permute-done.15.refs_2_, bf16[672,256]{1,0:T(8,128)(2,1)S(1)} %collective-permute-done.16.refs_3_, ...), custom_call_target="tpu_custom_call" | custom-call | flops 5637144576 | bytes 7340032 | tf_op jit(solution)/shard_map/down/pallas_call | solution.py:128
  217.4 1.8 copy-done.3
  219.2 11.5 %all-to-all-start.2 = ((bf16[128,8,1792]{2,1,0:T(8,128)(2,1)}), bf16[128,8,1792]{2,1,0:T(8,128)(2,1)}, u32[]{:S(2)}, u32[]{:S(2)}) async-start(bf16[128,8,1792]{2,1,0:T(8,128)(2,1)} %bitcast.54), calls=%async_computation.2 | async-start | bytes 7340032 | tf_op jit(solution)/shard_map/all_to_all | solution.py:198
  232.1 2.1 select_n.187
  234.2 1.5 copy.26.mixing_ref
  235.7 75.9 %all-to-all-done.2 = bf16[128,8,1792]{2,1,0:T(8,128)(2,1)} async-done(((bf16[128,8,1792]{2,1,0:T(8,128)(2,1)}), bf16[128,8,1792]{2,1,0:T(8,128)(2,1)}, u32[]{:S(2)}, u32[]{:S(2)}) %all-to-all-start.2) | async-done | bytes 3670048 | tf_op jit(solution)/shard_map/all_to_all | solution.py:198
  311.5 5.0 %mix.1 = bf16[64,7168]{1,0:T(8,128)(2,1)} custom-call(bf16[1024,1792]{1,0:T(8,128)(2,1)} %bitcast.15.returned_ref, bf16[512,1024]{1,0:T(8,128)(2,1)S(1)} %copy.26.mixing_ref, bf16[64,7168]{1,0:T(8,128)(2,1)S(1)} %bitcast.53), custom_call_target="tpu_custom_call" | custom-call | tf_op jit(solution)/shard_map/mix/pallas_call | solution.py:164
  (92 shorter events, 8.3 us)
Async XLA Ops:
  0.0 3.6 %copy-start.12 = (f32[1,7168]{1,0:T(1,128)S(1)}, f32[1,7168]{1,0:T(1,128)}, u32[]{:S(2)}) copy-start(f32[1,7168]{1,0:T(1,128)} %param.8) | copy-start | bytes 86020
  0.0 3.3 %collective-permute-start = (bf16[1,64,7168]{2,1,0:T(8,128)(2,1)}, bf16[1,64,7168]{2,1,0:T(8,128)(2,1)S(1)}, u32[]{:S(2)}, u32[]{:S(2)}) collective-permute-start(bf16[1,64,7168]{2,1,0:T(8,128)(2,1)} %param.7), channel_id=1, source_target_pairs={{0,128},{128,0},{1,129},{129,1},{2,130},{130,2},{3,131},{131,3},{4... | collective-permute-start | bytes 2752520 | tf_op jit(solution)/shard_map/ppermute | solution.py:210
  3.3 3.4 %copy-start.10 = (pred[1792,512]{1,0:T(8,128)(4,1)}, pred[1792,512]{1,0:T(8,128)(4,1)S(1)}, u32[]{:S(2)}) copy-start(pred[1792,512]{1,0:T(8,128)(4,1)S(1)} %compare_reduce_fusion) | copy-start | bytes 2752516
  6.7 59.0 %all-to-all-start.1 = ((bf16[32,56,512]{2,1,0:T(8,128)(2,1)}), bf16[32,56,512]{2,1,0:T(8,128)(2,1)}, u32[]{:S(2)}, u32[]{:S(2)}) async-start(bf16[32,56,512]{2,1,0:T(8,128)(2,1)} %bitcast.55), calls=%async_computation.1 | async-start | bytes 3670016 | tf_op jit(solution)/shard_map/all_to_all | solution.py:198
  18.0 7.8 %copy-start.11 = (pred[1792,512]{1,0:T(8,128)(4,1)S(1)}, pred[1792,512]{1,0:T(8,128)(4,1)}, u32[]{:S(2)}) copy-start(pred[1792,512]{1,0:T(8,128)(4,1)} %copy-done.10) | copy-start | bytes 2752516
  20.3 23.5 %collective-permute-start.1 = (bf16[256,1792]{1,0:T(8,128)(2,1)S(1)}, bf16[256,1792]{1,0:T(8,128)(2,1)S(1)}, u32[]{:S(2)}, u32[]{:S(2)}) collective-permute-start(bf16[256,1792]{1,0:T(8,128)(2,1)S(1)} %get-tuple-element.42), channel_id=1, source_target_pairs={{0,1},{1,2},{2,3},{3,0},{4,5},{5,6},{6,7},{7,4},{8,9},{9,10},{10,1... | collective-permute-start | bytes 2752520 | tf_op jit(solution)/shard_map/ppermute | solution.py:195
  22.0 40.9 %collective-permute-start.2 = (bf16[256,1792]{1,0:T(8,128)(2,1)S(1)}, bf16[256,1792]{1,0:T(8,128)(2,1)S(1)}, u32[]{:S(2)}, u32[]{:S(2)}) collective-permute-start(bf16[256,1792]{1,0:T(8,128)(2,1)S(1)} %get-tuple-element.44), channel_id=1, source_target_pairs={{0,3},{1,0},{2,1},{3,2},{4,7},{5,4},{6,5},{7,6},{8,11},{9,8},{10,9... | collective-permute-start | bytes 2752520 | tf_op jit(solution)/shard_map/ppermute | solution.py:195
  23.6 41.1 %collective-permute-start.3 = (bf16[256,1792]{1,0:T(8,128)(2,1)S(1)}, bf16[256,1792]{1,0:T(8,128)(2,1)S(1)}, u32[]{:S(2)}, u32[]{:S(2)}) collective-permute-start(bf16[256,1792]{1,0:T(8,128)(2,1)S(1)} %get-tuple-element.41), channel_id=1, source_target_pairs={{0,2},{1,3},{2,0},{3,1},{4,6},{5,7},{6,4},{7,5},{8,10},{9,11},{10,... | collective-permute-start | bytes 2752520 | tf_op jit(solution)/shard_map/ppermute | solution.py:195
  43.8 0.9 copy-start.4
  62.9 1.0 copy-start.6
  64.7 0.9 copy-start.8
  65.6 44.2 %all-to-all-start = ((bf16[32,56,384]{2,1,0:T(8,128)(2,1)}), bf16[32,56,384]{2,1,0:T(8,128)(2,1)}, u32[]{:S(2)}, u32[]{:S(2)}) async-start(bf16[32,56,384]{2,1,0:T(8,128)(2,1)} %bitcast.4), calls=%async_computation | async-start | bytes 2752512 | tf_op jit(solution)/shard_map/all_to_all | solution.py:198
  80.5 29.4 %collective-permute-start.4 = (bf16[112,4096]{1,0:T(8,128)(2,1)}, bf16[112,4096]{1,0:T(8,128)(2,1)}, u32[]{:S(2)}, u32[]{:S(2)}) collective-permute-start(bf16[112,4096]{1,0:T(8,128)(2,1)} %get-tuple-element.29.refs_0_), channel_id=1, source_target_pairs={{0,1},{1,2},{2,3},{3,0},{4,5},{5,6},{6,7},{7,4},{8,9},{9,10},{10,1... | collective-permute-start | bytes 2752520 | tf_op jit(solution)/shard_map/ppermute | solution.py:195
  81.6 28.2 %collective-permute-start.5 = (bf16[112,4096]{1,0:T(8,128)(2,1)}, bf16[112,4096]{1,0:T(8,128)(2,1)}, u32[]{:S(2)}, u32[]{:S(2)}) collective-permute-start(bf16[112,4096]{1,0:T(8,128)(2,1)} %get-tuple-element.30.refs_1_), channel_id=1, source_target_pairs={{0,3},{1,0},{2,1},{3,2},{4,7},{5,4},{6,5},{7,6},{8,11},{9,8},{10,9... | collective-permute-start | bytes 2752520 | tf_op jit(solution)/shard_map/ppermute | solution.py:195
  83.7 41.2 %collective-permute-start.10 = (bf16[112,4096]{1,0:T(8,128)(2,1)}, bf16[112,4096]{1,0:T(8,128)(2,1)}, u32[]{:S(2)}, u32[]{:S(2)}) collective-permute-start(bf16[112,4096]{1,0:T(8,128)(2,1)} %get-tuple-element.30.refs_1_), channel_id=1, source_target_pairs={{0,1},{1,2},{2,3},{3,0},{4,5},{5,6},{6,7},{7,4},{8,9},{9,10},{10,1... | collective-permute-start | bytes 2752520 | tf_op jit(solution)/shard_map/ppermute | solution.py:195
  83.7 42.9 %collective-permute-start.11 = (bf16[112,4096]{1,0:T(8,128)(2,1)}, bf16[112,4096]{1,0:T(8,128)(2,1)}, u32[]{:S(2)}, u32[]{:S(2)}) collective-permute-start(bf16[112,4096]{1,0:T(8,128)(2,1)} %get-tuple-element.29.refs_0_), channel_id=1, source_target_pairs={{0,3},{1,0},{2,1},{3,2},{4,7},{5,4},{6,5},{7,6},{8,11},{9,8},{10,9... | collective-permute-start | bytes 2752520 | tf_op jit(solution)/shard_map/ppermute | solution.py:195
  114.1 25.5 %collective-permute-start.6 = (bf16[112,3072]{1,0:T(8,128)(2,1)}, bf16[112,3072]{1,0:T(8,128)(2,1)S(1)}, u32[]{:S(2)}, u32[]{:S(2)}) collective-permute-start(bf16[112,3072]{1,0:T(8,128)(2,1)} %get-tuple-element.27.refs_0_), channel_id=1, source_target_pairs={{0,1},{1,2},{2,3},{3,0},{4,5},{5,6},{6,7},{7,4},{8,9},{9,10},{10,1... | collective-permute-start | bytes 2064392 | tf_op jit(solution)/shard_map/ppermute | solution.py:195
  114.9 45.8 %collective-permute-start.12 = (bf16[112,4096]{1,0:T(8,128)(2,1)}, bf16[112,4096]{1,0:T(8,128)(2,1)S(1)}, u32[]{:S(2)}, u32[]{:S(2)}) collective-permute-start(bf16[112,4096]{1,0:T(8,128)(2,1)} %collective-permute-done.4.refs_2_), channel_id=1, source_target_pairs={{0,1},{1,2},{2,3},{3,0},{4,5},{5,6},{6,7},{7,4},{8,9},{9,10},{10,1... | collective-permute-start | bytes 2752520 | tf_op jit(solution)/shard_map/ppermute | solution.py:195
  115.2 47.3 %collective-permute-start.13 = (bf16[112,4096]{1,0:T(8,128)(2,1)}, bf16[112,4096]{1,0:T(8,128)(2,1)S(1)}, u32[]{:S(2)}, u32[]{:S(2)}) collective-permute-start(bf16[112,4096]{1,0:T(8,128)(2,1)} %collective-permute-done.5.refs_5_), channel_id=1, source_target_pairs={{0,3},{1,0},{2,1},{3,2},{4,7},{5,4},{6,5},{7,6},{8,11},{9,8},{10,9... | collective-permute-start | bytes 2752520 | tf_op jit(solution)/shard_map/ppermute | solution.py:195
  125.0 34.2 %collective-permute-start.9 = (bf16[112,3072]{1,0:T(8,128)(2,1)}, bf16[112,3072]{1,0:T(8,128)(2,1)S(1)}, u32[]{:S(2)}, u32[]{:S(2)}) collective-permute-start(bf16[112,3072]{1,0:T(8,128)(2,1)} %get-tuple-element.28.refs_1_), channel_id=1, source_target_pairs={{0,3},{1,0},{2,1},{3,2},{4,7},{5,4},{6,5},{7,6},{8,11},{9,8},{10,9... | collective-permute-start | bytes 2064392 | tf_op jit(solution)/shard_map/ppermute | solution.py:195
  126.6 47.5 %collective-permute-start.7 = (bf16[112,3072]{1,0:T(8,128)(2,1)}, bf16[112,3072]{1,0:T(8,128)(2,1)}, u32[]{:S(2)}, u32[]{:S(2)}) collective-permute-start(bf16[112,3072]{1,0:T(8,128)(2,1)} %get-tuple-element.28.refs_1_), channel_id=1, source_target_pairs={{0,1},{1,2},{2,3},{3,0},{4,5},{5,6},{6,7},{7,4},{8,9},{9,10},{10,1... | collective-permute-start | bytes 2064392 | tf_op jit(solution)/shard_map/ppermute | solution.py:195
  139.6 34.5 %collective-permute-start.8 = (bf16[112,3072]{1,0:T(8,128)(2,1)}, bf16[112,3072]{1,0:T(8,128)(2,1)}, u32[]{:S(2)}, u32[]{:S(2)}) collective-permute-start(bf16[112,3072]{1,0:T(8,128)(2,1)} %get-tuple-element.27.refs_0_), channel_id=1, source_target_pairs={{0,3},{1,0},{2,1},{3,2},{4,7},{5,4},{6,5},{7,6},{8,11},{9,8},{10,9... | collective-permute-start | bytes 2064392 | tf_op jit(solution)/shard_map/ppermute | solution.py:195
  159.2 29.6 %collective-permute-start.17 = (bf16[112,3072]{1,0:T(8,128)(2,1)S(1)}, bf16[112,3072]{1,0:T(8,128)(2,1)S(1)}, u32[]{:S(2)}, u32[]{:S(2)}) collective-permute-start(bf16[112,3072]{1,0:T(8,128)(2,1)S(1)} %collective-permute-done.6.refs_2_), channel_id=1, source_target_pairs={{0,1},{1,2},{2,3},{3,0},{4,5},{5,6},{6,7},{7,4},{8,9},{9,10},{10,1... | collective-permute-start | bytes 2064392 | tf_op jit(solution)/shard_map/ppermute | solution.py:195
  160.7 28.1 %collective-permute-start.18 = (bf16[112,3072]{1,0:T(8,128)(2,1)S(1)}, bf16[112,3072]{1,0:T(8,128)(2,1)}, u32[]{:S(2)}, u32[]{:S(2)}) collective-permute-start(bf16[112,3072]{1,0:T(8,128)(2,1)S(1)} %collective-permute-done.9.refs_5_), channel_id=1, source_target_pairs={{0,3},{1,0},{2,1},{3,2},{4,7},{5,4},{6,5},{7,6},{8,11},{9,8},{10,9... | collective-permute-start | bytes 2064392 | tf_op jit(solution)/shard_map/ppermute | solution.py:195
  162.5 2.0 copy-start
  164.6 9.6 %copy-start.1 = (bf16[1,7168,256]{2,1,0:T(8,128)(2,1)S(1)}, bf16[1,7168,256]{2,1,0:T(8,128)(2,1)}, u32[]{:S(2)}) copy-start(bf16[1,7168,256]{2,1,0:T(8,128)(2,1)} %param.11) | copy-start | bytes 11010052
  164.6 9.6 %copy-start.2 = (bf16[1,7168,256]{2,1,0:T(8,128)(2,1)S(1)}, bf16[1,7168,256]{2,1,0:T(8,128)(2,1)}, u32[]{:S(2)}) copy-start(bf16[1,7168,256]{2,1,0:T(8,128)(2,1)} %param.12) | copy-start | bytes 11010052
  178.8 24.7 %collective-permute-start.14 = (bf16[672,256]{1,0:T(8,128)(2,1)S(1)}, bf16[672,256]{1,0:T(8,128)(2,1)S(1)}, u32[]{:S(2)}, u32[]{:S(2)}) collective-permute-start(bf16[672,256]{1,0:T(8,128)(2,1)S(1)} %gate_up.4.refs_0_), channel_id=1, source_target_pairs={{0,1},{1,2},{2,3},{3,0},{4,5},{5,6},{6,7},{7,4},{8,9},{9,10},{10,1... | collective-permute-start | bytes 1032200 | tf_op jit(solution)/shard_map/ppermute | solution.py:195
  180.3 23.9 %collective-permute-start.15 = (bf16[672,256]{1,0:T(8,128)(2,1)S(1)}, bf16[672,256]{1,0:T(8,128)(2,1)S(1)}, u32[]{:S(2)}, u32[]{:S(2)}) collective-permute-start(bf16[672,256]{1,0:T(8,128)(2,1)S(1)} %gate_up.4.refs_0_), channel_id=1, source_target_pairs={{0,3},{1,0},{2,1},{3,2},{4,7},{5,4},{6,5},{7,6},{8,11},{9,8},{10,9... | collective-permute-start | bytes 1032200 | tf_op jit(solution)/shard_map/ppermute | solution.py:195
  182.2 22.0 %collective-permute-start.16 = (bf16[672,256]{1,0:T(8,128)(2,1)S(1)}, bf16[672,256]{1,0:T(8,128)(2,1)S(1)}, u32[]{:S(2)}, u32[]{:S(2)}) collective-permute-start(bf16[672,256]{1,0:T(8,128)(2,1)S(1)} %gate_up.4.refs_0_), channel_id=1, source_target_pairs={{0,2},{1,3},{2,0},{3,1},{4,6},{5,7},{6,4},{7,5},{8,10},{9,11},{10,... | collective-permute-start | bytes 1032200 | tf_op jit(solution)/shard_map/ppermute | solution.py:195
  184.0 25.8 %copy-start.5 = (bf16[256,1792]{1,0:T(8,128)(2,1)S(1)}, bf16[256,1792]{1,0:T(8,128)(2,1)}, u32[]{:S(2)}) copy-start(bf16[256,1792]{1,0:T(8,128)(2,1)} %copy-done.4) | copy-start | bytes 2752516
  184.0 25.7 %copy-start.7 = (bf16[256,1792]{1,0:T(8,128)(2,1)S(1)}, bf16[256,1792]{1,0:T(8,128)(2,1)}, u32[]{:S(2)}) copy-start(bf16[256,1792]{1,0:T(8,128)(2,1)} %copy-done.6) | copy-start | bytes 2752516
  184.0 25.7 %copy-start.9 = (bf16[256,1792]{1,0:T(8,128)(2,1)S(1)}, bf16[256,1792]{1,0:T(8,128)(2,1)}, u32[]{:S(2)}) copy-start(bf16[256,1792]{1,0:T(8,128)(2,1)} %copy-done.8) | copy-start | bytes 2752516
  191.7 13.0 %collective-permute-start.19 = (bf16[224,256]{1,0:T(8,128)(2,1)S(1)}, bf16[224,256]{1,0:T(8,128)(2,1)S(1)}, u32[]{:S(2)}, u32[]{:S(2)}) collective-permute-start(bf16[224,256]{1,0:T(8,128)(2,1)S(1)} %gate_up.5.refs_4_), channel_id=1, source_target_pairs={{0,1},{1,2},{2,3},{3,0},{4,5},{5,6},{6,7},{7,4},{8,9},{9,10},{10,1... | collective-permute-start | bytes 344072 | tf_op jit(solution)/shard_map/ppermute | solution.py:195
  192.8 11.9 %collective-permute-start.20 = (bf16[224,256]{1,0:T(8,128)(2,1)S(1)}, bf16[224,256]{1,0:T(8,128)(2,1)S(1)}, u32[]{:S(2)}, u32[]{:S(2)}) collective-permute-start(bf16[224,256]{1,0:T(8,128)(2,1)S(1)} %gate_up.5.refs_4_), channel_id=1, source_target_pairs={{0,3},{1,0},{2,1},{3,2},{4,7},{5,4},{6,5},{7,6},{8,11},{9,8},{10,9... | collective-permute-start | bytes 344072 | tf_op jit(solution)/shard_map/ppermute | solution.py:195
  203.5 6.3 %collective-permute-start.21 = (bf16[224,256]{1,0:T(8,128)(2,1)S(1)}, bf16[224,256]{1,0:T(8,128)(2,1)S(1)}, u32[]{:S(2)}, u32[]{:S(2)}) collective-permute-start(bf16[224,256]{1,0:T(8,128)(2,1)S(1)} %gate_up.5.refs_4_), channel_id=1, source_target_pairs={{0,2},{1,3},{2,0},{3,1},{4,6},{5,7},{6,4},{7,5},{8,10},{9,11},{10,... | collective-permute-start | bytes 344072 | tf_op jit(solution)/shard_map/ppermute | solution.py:195
  217.4 1.8 copy-start.3
  219.2 11.5 %copy-start.13 = (f32[1,64,3]{1,0,2:T(1,128)S(1)}, f32[1,64,3]{1,0,2:T(1,128)}, u32[]{:S(2)}) copy-start(f32[1,64,3]{1,0,2:T(1,128)} %param.10) | copy-start | bytes 2308
  219.2 92.3 %all-to-all-start.2 = ((bf16[128,8,1792]{2,1,0:T(8,128)(2,1)}), bf16[128,8,1792]{2,1,0:T(8,128)(2,1)}, u32[]{:S(2)}, u32[]{:S(2)}) async-start(bf16[128,8,1792]{2,1,0:T(8,128)(2,1)} %bitcast.54), calls=%async_computation.2 | async-start | bytes 7340032 | tf_op jit(solution)/shard_map/all_to_all | solution.py:198

commit v2 on v1

--- a/solution.py
+++ b/solution.py
@@ -17,27 +17,33 @@
 epsilon = 1e-06
 
 
-def unfold_kernel(sort_ref, landed_ref, *out_refs):
+def unfold_kernel(parts, sort_ref, landed_ref, *out_refs):
     cols = landed_ref.shape[1]
-    rows = landed_ref.shape[0] // len(out_refs)
-    for h, out_ref in enumerate(out_refs):
-        count = out_ref.shape[0]
+    rows = sort_ref.shape[0]
+    count = out_refs[0].shape[0]
+    halves = len(out_refs) // parts
+    for h in range(halves):
         part = landed_ref[h * rows : (h + 1) * rows, :]
         sorted_part = jnp.dot(sort_ref[...], part, preferred_element_type=jnp.float32)
-        sorted_part = sorted_part.astype(out_ref.dtype)
-        for f in range(FOLD):
-            out_ref[:, f * cols : (f + 1) * cols] = sorted_part[f * count : (f + 1) * count]
-
-
-def unfold(landed, sort):
+        sorted_part = sorted_part.astype(landed_ref.dtype)
+        for q in range(rows // count):
+            fold, part_index = q // parts, q % parts
+            out_ref = out_refs[part_index * halves + h]
+            out_ref[:, fold * cols : (fold + 1) * cols] = sorted_part[q * count : (q + 1) * count]
+
+
+def unfold(landed, sort, count, parts):
     rows, cols = landed.shape
-    count = sort.shape[0] // FOLD
     halves = rows // sort.shape[0]
-    shape = jax.ShapeDtypeStruct((count, cols * FOLD), landed.dtype)
+    folds = sort.shape[0] // count // parts
+    shape = jax.ShapeDtypeStruct((count, cols * folds), landed.dtype)
     return pl.pallas_call(
-        unfold_kernel,
-        out_shape=[shape] * halves,
+        functools.partial(unfold_kernel, parts),
+        out_shape=[shape] * (halves * parts),
         compiler_params=pltpu.CompilerParams(vmem_limit_bytes=VMEM),
+        cost_estimate=pl.CostEstimate(
+            flops=2 * rows * cols * sort.shape[0], bytes_accessed=4 * landed.size, transcendentals=0
+        ),
         name="unfold",
     )(sort, landed)
 
@@ -250,7 +256,7 @@
         if c > 0:
             early = arrived[c - 1][2], arrived[c - 1][5]
             landed[c] = lax.optimization_barrier((landed[c], *early))[0]
-        first, second = unfold(landed[c], sort)
+        first, second = unfold(landed[c], sort, half, 1)
         left_first, right_second = shift(first, 1), shift(second, -1)
         left_second, right_first = shift(second, 1), shift(first, -1)
         far_first, far_second = shift(left_first, 1), shift(right_second, -1)

time: 317 us -> 318 us (level)
  local copies, waits for them, and re-layouts: 14.5 us -> 22 us
  Pallas kernels: 36.4 us -> 30.6 us
    unnamed x44 -> x50, local copies, waits for them, and re-layouts: 7.67 us -> 13.4 us
    pallas_call x3, Pallas kernels: 14.9 us -> 11.5 us  [gate_up(): pl.pallas_call(functools.partial(gate_up_kernel, len(pieces), steps, last...]
  transfers between devices with their start and end apart: 25 -> 25, of which waited for: 13 -> 13; matrix products, arithmetic and copies ran while one was open for 4% -> 7% of each run, Pallas kernels for 8% -> 6%
where the time goes in v2:
time: 318 us; the launch traced here: 317 us
  waiting for transfers between devices  190 us (60%)
  starting transfers between devices  63.6 us (20%)
  Pallas kernels  30.6 us (10%)
  local copies, waits for them, and re-layouts  22 us (7%)
  matrix products  5.12 us (2%)
  other arithmetic  4.5 us (1%)
    all_to_all x3, waiting for transfers between devices, exchange(): lax.all_to_all(block, 'expert', split_axis=0, concat_axis=0, axis_index_g...  100 us
    ppermute x21, waiting for transfers between devices, shift(): return lax.ppermute(block, 'expert', route)  90 us
    all_to_all x3, starting transfers between devices, exchange(): lax.all_to_all(block, 'expert', split_axis=0, concat_axis=0, axis_index_g...  32.5 us
    ppermute x21, starting transfers between devices, shift(): return lax.ppermute(block, 'expert', route)  31.1 us
    unnamed x50, local copies, waits for them, and re-layouts  13.4 us
    pallas_call x3, Pallas kernels, gate_up(): pl.pallas_call(functools.partial(gate_up_kernel, len(pieces), steps, last...  11.5 us
    pallas_call x1, Pallas kernels, down(): pl.pallas_call(functools.partial(down_kernel, orders), grid=(width // col...  7.63 us
    pallas_call x2, Pallas kernels, unfold(): pl.pallas_call(functools.partial(unfold_kernel, parts), out_shape=[shape]...  6.58 us
  transfers between devices with their start and end apart: 25, of which 13 were waited for; matrix products, arithmetic and copies ran while one was open for 7% of the time, Pallas kernels for 6%

profile of v2, /device:TPU:32, one launch (start us, length us, event | category | flops | bytes accessed | tf_op | source)
XLA Modules:
  0.0 316.6 jit_solution(12837714921269996756)
XLA Ops:
  2.3 1.0 compare_reduce_fusion
  4.8 2.6 convolution_convert_fusion
  7.4 11.2 %all-to-all-start.1 = ((bf16[32,56,512]{2,1,0:T(8,128)(2,1)}), bf16[32,56,512]{2,1,0:T(8,128)(2,1)S(1)}, u32[]{:S(2)}, u32[]{:S(2)}) async-start(bf16[32,56,512]{2,1,0:T(8,128)(2,1)} %bitcast.56), calls=%async_computation.1 | async-start | bytes 3670016 | tf_op jit(solution)/shard_map/all_to_all | solution.py:204
  18.7 3.3 %dynamic-slice_bitcast_fusion = (bf16[256,1792]{1,0:T(8,128)(2,1)S(1)}, bf16[256,1792]{1,0:T(8,128)(2,1)S(1)}, bf16[256,1792]{1,0:T(8,128)(2,1)}, bf16[256,1792]{1,0:T(8,128)(2,1)S(1)}) fusion(bf16[1,256,7168]{2,1,0:T(8,128)(2,1)} %param.13, s32[]{:T(128)S(6)} %select_n.177, s32[]{:T(128)S(6)} %select_n.175, s32[]{:T(128)S(6)} %select_n.174, s32[]{:T(128)S(6)} %select_n.176), kind=kLoop, calls=%fused_computation.18 | loop fusion | bytes 7340048 | tf_op jit(solution)/shard_map/dynamic_slice | solution.py:210
  22.0 1.6 collective-permute-start.1
  23.5 1.7 collective-permute-start.2
  25.2 2.0 collective-permute-start.3
  33.7 2.5 convolution_convert_fusion.1
  36.2 9.2 %collective-permute-done.1.refs_9_ = bf16[256,1792]{1,0:T(8,128)(2,1)S(1)} collective-permute-done((bf16[256,1792]{1,0:T(8,128)(2,1)S(1)}, bf16[256,1792]{1,0:T(8,128)(2,1)S(1)}, u32[]{:S(2)}, u32[]{:S(2)}) %collective-permute-start.1) | collective-permute-done | bytes 917536 | tf_op jit(solution)/shard_map/ppermute | solution.py:201
  45.4 0.9 copy-done.6
  46.8 0.9 copy-done.8
  47.8 18.5 %collective-permute-done.3.refs_11_ = bf16[256,1792]{1,0:T(8,128)(2,1)S(1)} collective-permute-done((bf16[256,1792]{1,0:T(8,128)(2,1)S(1)}, bf16[256,1792]{1,0:T(8,128)(2,1)S(1)}, u32[]{:S(2)}, u32[]{:S(2)}) %collective-permute-start.3) | collective-permute-done | bytes 917536 | tf_op jit(solution)/shard_map/ppermute | solution.py:201
  66.3 0.9 copy-done.10
  67.2 9.8 %all-to-all-start = ((bf16[32,56,384]{2,1,0:T(8,128)(2,1)}), bf16[32,56,384]{2,1,0:T(8,128)(2,1)}, u32[]{:S(2)}, u32[]{:S(2)}) async-start(bf16[32,56,384]{2,1,0:T(8,128)(2,1)} %bitcast.57), calls=%async_computation | async-start | bytes 2752512 | tf_op jit(solution)/shard_map/all_to_all | solution.py:204
  77.4 3.2 unfold.2
  80.6 1.1 collective-permute-start.4
  81.7 2.1 collective-permute-start.5
  83.8 3.2 %collective-permute-start.11 = (bf16[112,4096]{1,0:T(8,128)(2,1)}, bf16[112,4096]{1,0:T(8,128)(2,1)}, u32[]{:S(2)}, u32[]{:S(2)}) collective-permute-start(bf16[112,4096]{1,0:T(8,128)(2,1)} %get-tuple-element.29.refs_0_), channel_id=1, source_target_pairs={{0,3},{1,0},{2,1},{3,2},{4,7},{5,4},{6,5},{7,6},{8,11},{9,8},{10,9... | collective-permute-start | bytes 2752520 | tf_op jit(solution)/shard_map/ppermute | solution.py:201
  87.1 24.4 %all-to-all-done = bf16[32,56,384]{2,1,0:T(8,128)(2,1)} async-done(((bf16[32,56,384]{2,1,0:T(8,128)(2,1)}), bf16[32,56,384]{2,1,0:T(8,128)(2,1)}, u32[]{:S(2)}, u32[]{:S(2)}) %all-to-all-start) | async-done | bytes 1376288 | tf_op jit(solution)/shard_map/all_to_all | solution.py:204
  111.4 1.4 copy-done.4
  112.9 3.4 %unfold.3 = (bf16[112,3072]{1,0:T(8,128)(2,1)S(1)}, bf16[112,3072]{1,0:T(8,128)(2,1)S(1)}) custom-call(bf16[896,896]{1,0:T(8,128)(2,1)S(1)} %copy-done.4, bf16[1792,384]{1,0:T(8,128)(2,1)} %bitcast.9.landed_ref), custom_call_target="tpu_custom_call" | custom-call | flops 1233125376 | bytes 2752512 | tf_op jit(solution)/shard_map/unfold/pallas_call | solution.py:40
  116.3 0.9 collective-permute-start.6
  117.5 2.9 collective-permute-start.13
  120.4 4.7 %collective-permute-done.10.refs_3_ = bf16[112,4096]{1,0:T(8,128)(2,1)} collective-permute-done((bf16[112,4096]{1,0:T(8,128)(2,1)}, bf16[112,4096]{1,0:T(8,128)(2,1)}, u32[]{:S(2)}, u32[]{:S(2)}) %collective-permute-start.10) | collective-permute-done | bytes 917536 | tf_op jit(solution)/shard_map/ppermute | solution.py:201
  125.1 1.5 collective-permute-start.9
  127.1 12.6 %collective-permute-done.6.refs_2_ = bf16[112,3072]{1,0:T(8,128)(2,1)S(1)} collective-permute-done((bf16[112,3072]{1,0:T(8,128)(2,1)S(1)}, bf16[112,3072]{1,0:T(8,128)(2,1)S(1)}, u32[]{:S(2)}, u32[]{:S(2)}) %collective-permute-start.6) | collective-permute-done | bytes 688160 | tf_op jit(solution)/shard_map/ppermute | solution.py:201
  139.7 1.5 collective-permute-start.8
  141.2 18.1 %collective-permute-done.9.refs_5_ = bf16[112,3072]{1,0:T(8,128)(2,1)S(1)} collective-permute-done((bf16[112,3072]{1,0:T(8,128)(2,1)S(1)}, bf16[112,3072]{1,0:T(8,128)(2,1)S(1)}, u32[]{:S(2)}, u32[]{:S(2)}) %collective-permute-start.9) | collective-permute-done | bytes 688160 | tf_op jit(solution)/shard_map/ppermute | solution.py:201
  159.3 0.9 collective-permute-start.17
  160.2 2.4 collective-permute-start.18
  162.6 6.7 %gate_up.3.refs_8_.refs_4_ = f32[896,512]{1,0:T(8,128)S(1)} custom-call(bf16[112,4096]{1,0:T(8,128)(2,1)} %get-tuple-element.29.refs_0_, bf16[112,4096]{1,0:T(8,128)(2,1)} %get-tuple-element.30.refs_1_, bf16[112,4096]{1,0:T(8,128)(2,1)S(1)} %collective-permute-done.4.refs_2_, bf16[112,4096]{1,0:T(8,128)(2,1)} %collective-permute-done.10.refs_3_, ...), custom_call_target="tpu_custom_call" | custom-call | flops 3758096384 | bytes 11534336 | tf_op jit(solution)/shard_map/gate_up/pallas_call | solution.py:89
  169.3 4.8 %collective-permute-done.7.refs_3_ = bf16[112,3072]{1,0:T(8,128)(2,1)S(1)} collective-permute-done((bf16[112,3072]{1,0:T(8,128)(2,1)S(1)}, bf16[112,3072]{1,0:T(8,128)(2,1)S(1)}, u32[]{:S(2)}, u32[]{:S(2)}) %collective-permute-start.7) | collective-permute-done | bytes 688160 | tf_op jit(solution)/shard_map/ppermute | solution.py:201
  174.1 3.3 %gate_up.4.refs_0_ = bf16[672,256]{1,0:T(8,128)(2,1)S(1)} custom-call(bf16[112,3072]{1,0:T(8,128)(2,1)S(1)} %get-tuple-element.27.refs_0_, bf16[112,3072]{1,0:T(8,128)(2,1)S(1)} %get-tuple-element.28.refs_1_, bf16[112,3072]{1,0:T(8,128)(2,1)S(1)} %collective-permute-done.6.refs_2_, bf16[112,3072]{1,0:T(8,128)(2,1)S(1)} %collective-permute-done.7.refs_3_, ...), custom_call_target="tpu_custom_call" | custom-call | flops 2113929216 | bytes 7274496 | tf_op jit(solution)/shard_map/gate_up/pallas_call | solution.py:89
  178.3 2.5 collective-permute-start.15
  180.8 1.4 collective-permute-start.16
  182.3 6.6 %collective-permute-done.17.refs_0_ = bf16[112,3072]{1,0:T(8,128)(2,1)S(1)} collective-permute-done((bf16[112,3072]{1,0:T(8,128)(2,1)S(1)}, bf16[112,3072]{1,0:T(8,128)(2,1)S(1)}, u32[]{:S(2)}, u32[]{:S(2)}) %collective-permute-start.17) | collective-permute-done | bytes 688160 | tf_op jit(solution)/shard_map/ppermute | solution.py:201
  188.9 1.5 gate_up.5.refs_4_
  190.3 1.1 collective-permute-start.19
  191.4 2.6 collective-permute-start.20
  194.0 9.6 %collective-permute-done.14.refs_1_ = bf16[672,256]{1,0:T(8,128)(2,1)S(1)} collective-permute-done((bf16[672,256]{1,0:T(8,128)(2,1)S(1)}, bf16[672,256]{1,0:T(8,128)(2,1)S(1)}, u32[]{:S(2)}, u32[]{:S(2)}) %collective-permute-start.14) | collective-permute-done | bytes 344096 | tf_op jit(solution)/shard_map/ppermute | solution.py:201
  204.8 5.1 %collective-permute-done.21.refs_7_ = bf16[224,256]{1,0:T(8,128)(2,1)S(1)} collective-permute-done((bf16[224,256]{1,0:T(8,128)(2,1)S(1)}, bf16[224,256]{1,0:T(8,128)(2,1)S(1)}, u32[]{:S(2)}, u32[]{:S(2)}) %collective-permute-start.21) | collective-permute-done | bytes 114720 | tf_op jit(solution)/shard_map/ppermute | solution.py:201
  209.9 7.6 %down.1 = bf16[1024,1792]{1,0:T(8,128)(2,1)S(1)} custom-call(bf16[672,256]{1,0:T(8,128)(2,1)S(1)} %gate_up.4.refs_0_, bf16[672,256]{1,0:T(8,128)(2,1)S(1)} %collective-permute-done.14.refs_1_, bf16[672,256]{1,0:T(8,128)(2,1)S(1)} %collective-permute-done.15.refs_2_, bf16[672,256]{1,0:T(8,128)(2,1)S(1)} %collective-permute-done.16.refs_3_, ...), custom_call_target="tpu_custom_call" | custom-call | flops 5637144576 | bytes 7340032 | tf_op jit(solution)/shard_map/down/pallas_call | solution.py:134
  217.5 1.8 copy-done.2
  219.3 11.5 %all-to-all-start.2 = ((bf16[128,8,1792]{2,1,0:T(8,128)(2,1)}), bf16[128,8,1792]{2,1,0:T(8,128)(2,1)}, u32[]{:S(2)}, u32[]{:S(2)}) async-start(bf16[128,8,1792]{2,1,0:T(8,128)(2,1)} %bitcast.54), calls=%async_computation.2 | async-start | bytes 7340032 | tf_op jit(solution)/shard_map/all_to_all | solution.py:204
  232.2 2.1 select_n.187
  234.3 1.5 copy.26.mixing_ref
  235.8 75.9 %all-to-all-done.2 = bf16[128,8,1792]{2,1,0:T(8,128)(2,1)} async-done(((bf16[128,8,1792]{2,1,0:T(8,128)(2,1)}), bf16[128,8,1792]{2,1,0:T(8,128)(2,1)}, u32[]{:S(2)}, u32[]{:S(2)}) %all-to-all-start.2) | async-done | bytes 3670048 | tf_op jit(solution)/shard_map/all_to_all | solution.py:204
  311.6 5.0 %mix.1 = bf16[64,7168]{1,0:T(8,128)(2,1)} custom-call(bf16[1024,1792]{1,0:T(8,128)(2,1)} %bitcast.15.returned_ref, bf16[512,1024]{1,0:T(8,128)(2,1)S(1)} %copy.26.mixing_ref, bf16[64,7168]{1,0:T(8,128)(2,1)S(1)} %bitcast.53), custom_call_target="tpu_custom_call" | custom-call | tf_op jit(solution)/shard_map/mix/pallas_call | solution.py:170
  (98 shorter events, 15.2 us)
Async XLA Ops:
  0.0 3.6 %copy-start.15 = (f32[1,7168]{1,0:T(1,128)S(1)}, f32[1,7168]{1,0:T(1,128)}, u32[]{:S(2)}) copy-start(f32[1,7168]{1,0:T(1,128)} %param.8) | copy-start | bytes 86020
  0.0 3.3 %collective-permute-start = (bf16[1,64,7168]{2,1,0:T(8,128)(2,1)}, bf16[1,64,7168]{2,1,0:T(8,128)(2,1)S(1)}, u32[]{:S(2)}, u32[]{:S(2)}) collective-permute-start(bf16[1,64,7168]{2,1,0:T(8,128)(2,1)} %param.7), channel_id=1, source_target_pairs={{0,128},{128,0},{1,129},{129,1},{2,130},{130,2},{3,131},{131,3},{4... | collective-permute-start | bytes 2752520 | tf_op jit(solution)/shard_map/ppermute | solution.py:216
  3.3 4.1 %copy-start.13 = (pred[1792,512]{1,0:T(8,128)(4,1)}, pred[1792,512]{1,0:T(8,128)(4,1)S(1)}, u32[]{:S(2)}) copy-start(pred[1792,512]{1,0:T(8,128)(4,1)S(1)} %compare_reduce_fusion) | copy-start | bytes 2752516
  3.9 0.9 copy-start.12
  7.4 59.8 %all-to-all-start.1 = ((bf16[32,56,512]{2,1,0:T(8,128)(2,1)}), bf16[32,56,512]{2,1,0:T(8,128)(2,1)S(1)}, u32[]{:S(2)}, u32[]{:S(2)}) async-start(bf16[32,56,512]{2,1,0:T(8,128)(2,1)} %bitcast.56), calls=%async_computation.1 | async-start | bytes 3670016 | tf_op jit(solution)/shard_map/all_to_all | solution.py:204
  18.7 15.0 %copy-start.14 = (pred[1792,512]{1,0:T(8,128)(4,1)S(1)}, pred[1792,512]{1,0:T(8,128)(4,1)}, u32[]{:S(2)}) copy-start(pred[1792,512]{1,0:T(8,128)(4,1)} %copy-done.13) | copy-start | bytes 2752516
  22.0 23.5 %collective-permute-start.1 = (bf16[256,1792]{1,0:T(8,128)(2,1)S(1)}, bf16[256,1792]{1,0:T(8,128)(2,1)S(1)}, u32[]{:S(2)}, u32[]{:S(2)}) collective-permute-start(bf16[256,1792]{1,0:T(8,128)(2,1)S(1)} %get-tuple-element.42), channel_id=1, source_target_pairs={{0,1},{1,2},{2,3},{3,0},{4,5},{5,6},{6,7},{7,4},{8,9},{9,10},{10,1... | collective-permute-start | bytes 2752520 | tf_op jit(solution)/shard_map/ppermute | solution.py:201
  23.5 23.3 %collective-permute-start.2 = (bf16[256,1792]{1,0:T(8,128)(2,1)S(1)}, bf16[256,1792]{1,0:T(8,128)(2,1)S(1)}, u32[]{:S(2)}, u32[]{:S(2)}) collective-permute-start(bf16[256,1792]{1,0:T(8,128)(2,1)S(1)} %get-tuple-element.44), channel_id=1, source_target_pairs={{0,3},{1,0},{2,1},{3,2},{4,7},{5,4},{6,5},{7,6},{8,11},{9,8},{10,9... | collective-permute-start | bytes 2752520 | tf_op jit(solution)/shard_map/ppermute | solution.py:201
  25.2 41.1 %collective-permute-start.3 = (bf16[256,1792]{1,0:T(8,128)(2,1)S(1)}, bf16[256,1792]{1,0:T(8,128)(2,1)S(1)}, u32[]{:S(2)}, u32[]{:S(2)}) collective-permute-start(bf16[256,1792]{1,0:T(8,128)(2,1)S(1)} %get-tuple-element.41), channel_id=1, source_target_pairs={{0,2},{1,3},{2,0},{3,1},{4,6},{5,7},{6,4},{7,5},{8,10},{9,11},{10,... | collective-permute-start | bytes 2752520 | tf_op jit(solution)/shard_map/ppermute | solution.py:201
  45.4 0.9 copy-start.6
  46.8 0.9 copy-start.8
  66.3 0.9 copy-start.10
  67.2 44.2 %all-to-all-start = ((bf16[32,56,384]{2,1,0:T(8,128)(2,1)}), bf16[32,56,384]{2,1,0:T(8,128)(2,1)}, u32[]{:S(2)}, u32[]{:S(2)}) async-start(bf16[32,56,384]{2,1,0:T(8,128)(2,1)} %bitcast.57), calls=%async_computation | async-start | bytes 2752512 | tf_op jit(solution)/shard_map/all_to_all | solution.py:204
  77.4 3.2 copy-start.3
  80.6 30.8 %collective-permute-start.4 = (bf16[112,4096]{1,0:T(8,128)(2,1)}, bf16[112,4096]{1,0:T(8,128)(2,1)S(1)}, u32[]{:S(2)}, u32[]{:S(2)}) collective-permute-start(bf16[112,4096]{1,0:T(8,128)(2,1)} %get-tuple-element.29.refs_0_), channel_id=1, source_target_pairs={{0,1},{1,2},{2,3},{3,0},{4,5},{5,6},{6,7},{7,4},{8,9},{9,10},{10,1... | collective-permute-start | bytes 2752520 | tf_op jit(solution)/shard_map/ppermute | solution.py:201
  81.7 29.7 %collective-permute-start.5 = (bf16[112,4096]{1,0:T(8,128)(2,1)}, bf16[112,4096]{1,0:T(8,128)(2,1)S(1)}, u32[]{:S(2)}, u32[]{:S(2)}) collective-permute-start(bf16[112,4096]{1,0:T(8,128)(2,1)} %get-tuple-element.30.refs_1_), channel_id=1, source_target_pairs={{0,3},{1,0},{2,1},{3,2},{4,7},{5,4},{6,5},{7,6},{8,11},{9,8},{10,9... | collective-permute-start | bytes 2752520 | tf_op jit(solution)/shard_map/ppermute | solution.py:201
  83.8 41.2 %collective-permute-start.10 = (bf16[112,4096]{1,0:T(8,128)(2,1)}, bf16[112,4096]{1,0:T(8,128)(2,1)}, u32[]{:S(2)}, u32[]{:S(2)}) collective-permute-start(bf16[112,4096]{1,0:T(8,128)(2,1)} %get-tuple-element.30.refs_1_), channel_id=1, source_target_pairs={{0,1},{1,2},{2,3},{3,0},{4,5},{5,6},{6,7},{7,4},{8,9},{9,10},{10,1... | collective-permute-start | bytes 2752520 | tf_op jit(solution)/shard_map/ppermute | solution.py:201
  83.8 42.7 %collective-permute-start.11 = (bf16[112,4096]{1,0:T(8,128)(2,1)}, bf16[112,4096]{1,0:T(8,128)(2,1)}, u32[]{:S(2)}, u32[]{:S(2)}) collective-permute-start(bf16[112,4096]{1,0:T(8,128)(2,1)} %get-tuple-element.29.refs_0_), channel_id=1, source_target_pairs={{0,3},{1,0},{2,1},{3,2},{4,7},{5,4},{6,5},{7,6},{8,11},{9,8},{10,9... | collective-permute-start | bytes 2752520 | tf_op jit(solution)/shard_map/ppermute | solution.py:201
  111.4 1.4 copy-start.4
  112.8 49.8 %copy-start = (bf16[1,7168,256]{2,1,0:T(8,128)(2,1)S(1)}, bf16[1,7168,256]{2,1,0:T(8,128)(2,1)}, u32[]{:S(2)}) copy-start(bf16[1,7168,256]{2,1,0:T(8,128)(2,1)} %param.11) | copy-start | bytes 11010052
  116.3 23.4 %collective-permute-start.6 = (bf16[112,3072]{1,0:T(8,128)(2,1)S(1)}, bf16[112,3072]{1,0:T(8,128)(2,1)S(1)}, u32[]{:S(2)}, u32[]{:S(2)}) collective-permute-start(bf16[112,3072]{1,0:T(8,128)(2,1)S(1)} %get-tuple-element.27.refs_0_), channel_id=1, source_target_pairs={{0,1},{1,2},{2,3},{3,0},{4,5},{5,6},{6,7},{7,4},{8,9},{9,10},{10,1... | collective-permute-start | bytes 2064392 | tf_op jit(solution)/shard_map/ppermute | solution.py:201
  117.2 43.0 %collective-permute-start.12 = (bf16[112,4096]{1,0:T(8,128)(2,1)S(1)}, bf16[112,4096]{1,0:T(8,128)(2,1)S(1)}, u32[]{:S(2)}, u32[]{:S(2)}) collective-permute-start(bf16[112,4096]{1,0:T(8,128)(2,1)S(1)} %collective-permute-done.4.refs_2_), channel_id=1, source_target_pairs={{0,1},{1,2},{2,3},{3,0},{4,5},{5,6},{6,7},{7,4},{8,9},{9,10},{10,1... | collective-permute-start | bytes 2752520 | tf_op jit(solution)/shard_map/ppermute | solution.py:201
  117.5 45.2 %collective-permute-start.13 = (bf16[112,4096]{1,0:T(8,128)(2,1)S(1)}, bf16[112,4096]{1,0:T(8,128)(2,1)S(1)}, u32[]{:S(2)}, u32[]{:S(2)}) collective-permute-start(bf16[112,4096]{1,0:T(8,128)(2,1)S(1)} %collective-permute-done.5.refs_5_), channel_id=1, source_target_pairs={{0,3},{1,0},{2,1},{3,2},{4,7},{5,4},{6,5},{7,6},{8,11},{9,8},{10,9... | collective-permute-start | bytes 2752520 | tf_op jit(solution)/shard_map/ppermute | solution.py:201
  125.1 34.2 %collective-permute-start.9 = (bf16[112,3072]{1,0:T(8,128)(2,1)S(1)}, bf16[112,3072]{1,0:T(8,128)(2,1)S(1)}, u32[]{:S(2)}, u32[]{:S(2)}) collective-permute-start(bf16[112,3072]{1,0:T(8,128)(2,1)S(1)} %get-tuple-element.28.refs_1_), channel_id=1, source_target_pairs={{0,3},{1,0},{2,1},{3,2},{4,7},{5,4},{6,5},{7,6},{8,11},{9,8},{10,9... | collective-permute-start | bytes 2064392 | tf_op jit(solution)/shard_map/ppermute | solution.py:201
  126.6 47.5 %collective-permute-start.7 = (bf16[112,3072]{1,0:T(8,128)(2,1)S(1)}, bf16[112,3072]{1,0:T(8,128)(2,1)S(1)}, u32[]{:S(2)}, u32[]{:S(2)}) collective-permute-start(bf16[112,3072]{1,0:T(8,128)(2,1)S(1)} %get-tuple-element.28.refs_1_), channel_id=1, source_target_pairs={{0,1},{1,2},{2,3},{3,0},{4,5},{5,6},{6,7},{7,4},{8,9},{9,10},{10,1... | collective-permute-start | bytes 2064392 | tf_op jit(solution)/shard_map/ppermute | solution.py:201
  139.7 34.4 %collective-permute-start.8 = (bf16[112,3072]{1,0:T(8,128)(2,1)S(1)}, bf16[112,3072]{1,0:T(8,128)(2,1)S(1)}, u32[]{:S(2)}, u32[]{:S(2)}) collective-permute-start(bf16[112,3072]{1,0:T(8,128)(2,1)S(1)} %get-tuple-element.27.refs_0_), channel_id=1, source_target_pairs={{0,3},{1,0},{2,1},{3,2},{4,7},{5,4},{6,5},{7,6},{8,11},{9,8},{10,9... | collective-permute-start | bytes 2064392 | tf_op jit(solution)/shard_map/ppermute | solution.py:201
  159.3 29.6 %collective-permute-start.17 = (bf16[112,3072]{1,0:T(8,128)(2,1)S(1)}, bf16[112,3072]{1,0:T(8,128)(2,1)S(1)}, u32[]{:S(2)}, u32[]{:S(2)}) collective-permute-start(bf16[112,3072]{1,0:T(8,128)(2,1)S(1)} %collective-permute-done.6.refs_2_), channel_id=1, source_target_pairs={{0,1},{1,2},{2,3},{3,0},{4,5},{5,6},{6,7},{7,4},{8,9},{9,10},{10,1... | collective-permute-start | bytes 2064392 | tf_op jit(solution)/shard_map/ppermute | solution.py:201
  160.2 28.7 %collective-permute-start.18 = (bf16[112,3072]{1,0:T(8,128)(2,1)S(1)}, bf16[112,3072]{1,0:T(8,128)(2,1)S(1)}, u32[]{:S(2)}, u32[]{:S(2)}) collective-permute-start(bf16[112,3072]{1,0:T(8,128)(2,1)S(1)} %collective-permute-done.9.refs_5_), channel_id=1, source_target_pairs={{0,3},{1,0},{2,1},{3,2},{4,7},{5,4},{6,5},{7,6},{8,11},{9,8},{10,9... | collective-permute-start | bytes 2064392 | tf_op jit(solution)/shard_map/ppermute | solution.py:201
  162.6 11.5 %copy-start.1 = (bf16[1,7168,256]{2,1,0:T(8,128)(2,1)S(1)}, bf16[1,7168,256]{2,1,0:T(8,128)(2,1)}, u32[]{:S(2)}) copy-start(bf16[1,7168,256]{2,1,0:T(8,128)(2,1)} %param.12) | copy-start | bytes 11010052
  177.4 26.1 %collective-permute-start.14 = (bf16[672,256]{1,0:T(8,128)(2,1)S(1)}, bf16[672,256]{1,0:T(8,128)(2,1)S(1)}, u32[]{:S(2)}, u32[]{:S(2)}) collective-permute-start(bf16[672,256]{1,0:T(8,128)(2,1)S(1)} %gate_up.4.refs_0_), channel_id=1, source_target_pairs={{0,1},{1,2},{2,3},{3,0},{4,5},{5,6},{6,7},{7,4},{8,9},{9,10},{10,1... | collective-permute-start | bytes 1032200 | tf_op jit(solution)/shard_map/ppermute | solution.py:201
  178.3 25.9 %collective-permute-start.15 = (bf16[672,256]{1,0:T(8,128)(2,1)S(1)}, bf16[672,256]{1,0:T(8,128)(2,1)S(1)}, u32[]{:S(2)}, u32[]{:S(2)}) collective-permute-start(bf16[672,256]{1,0:T(8,128)(2,1)S(1)} %gate_up.4.refs_0_), channel_id=1, source_target_pairs={{0,3},{1,0},{2,1},{3,2},{4,7},{5,4},{6,5},{7,6},{8,11},{9,8},{10,9... | collective-permute-start | bytes 1032200 | tf_op jit(solution)/shard_map/ppermute | solution.py:201
  180.8 23.4 %collective-permute-start.16 = (bf16[672,256]{1,0:T(8,128)(2,1)S(1)}, bf16[672,256]{1,0:T(8,128)(2,1)S(1)}, u32[]{:S(2)}, u32[]{:S(2)}) collective-permute-start(bf16[672,256]{1,0:T(8,128)(2,1)S(1)} %gate_up.4.refs_0_), channel_id=1, source_target_pairs={{0,2},{1,3},{2,0},{3,1},{4,6},{5,7},{6,4},{7,5},{8,10},{9,11},{10,... | collective-permute-start | bytes 1032200 | tf_op jit(solution)/shard_map/ppermute | solution.py:201
  182.3 27.6 %copy-start.5 = (bf16[256,1792]{1,0:T(8,128)(2,1)S(1)}, bf16[256,1792]{1,0:T(8,128)(2,1)}, u32[]{:S(2)}) copy-start(bf16[256,1792]{1,0:T(8,128)(2,1)} %get-tuple-element.37.refs_8_) | copy-start | bytes 2752516
  182.3 27.6 %copy-start.7 = (bf16[256,1792]{1,0:T(8,128)(2,1)S(1)}, bf16[256,1792]{1,0:T(8,128)(2,1)}, u32[]{:S(2)}) copy-start(bf16[256,1792]{1,0:T(8,128)(2,1)} %copy-done.6) | copy-start | bytes 2752516
  182.3 27.6 %copy-start.9 = (bf16[256,1792]{1,0:T(8,128)(2,1)S(1)}, bf16[256,1792]{1,0:T(8,128)(2,1)}, u32[]{:S(2)}) copy-start(bf16[256,1792]{1,0:T(8,128)(2,1)} %copy-done.8) | copy-start | bytes 2752516
  182.3 27.6 %copy-start.11 = (bf16[256,1792]{1,0:T(8,128)(2,1)S(1)}, bf16[256,1792]{1,0:T(8,128)(2,1)}, u32[]{:S(2)}) copy-start(bf16[256,1792]{1,0:T(8,128)(2,1)} %copy-done.10) | copy-start | bytes 2752516
  190.3 14.4 %collective-permute-start.19 = (bf16[224,256]{1,0:T(8,128)(2,1)S(1)}, bf16[224,256]{1,0:T(8,128)(2,1)S(1)}, u32[]{:S(2)}, u32[]{:S(2)}) collective-permute-start(bf16[224,256]{1,0:T(8,128)(2,1)S(1)} %gate_up.5.refs_4_), channel_id=1, source_target_pairs={{0,1},{1,2},{2,3},{3,0},{4,5},{5,6},{6,7},{7,4},{8,9},{9,10},{10,1... | collective-permute-start | bytes 344072 | tf_op jit(solution)/shard_map/ppermute | solution.py:201
  191.4 13.4 %collective-permute-start.20 = (bf16[224,256]{1,0:T(8,128)(2,1)S(1)}, bf16[224,256]{1,0:T(8,128)(2,1)S(1)}, u32[]{:S(2)}, u32[]{:S(2)}) collective-permute-start(bf16[224,256]{1,0:T(8,128)(2,1)S(1)} %gate_up.5.refs_4_), channel_id=1, source_target_pairs={{0,3},{1,0},{2,1},{3,2},{4,7},{5,4},{6,5},{7,6},{8,11},{9,8},{10,9... | collective-permute-start | bytes 344072 | tf_op jit(solution)/shard_map/ppermute | solution.py:201
  203.5 6.3 %collective-permute-start.21 = (bf16[224,256]{1,0:T(8,128)(2,1)S(1)}, bf16[224,256]{1,0:T(8,128)(2,1)S(1)}, u32[]{:S(2)}, u32[]{:S(2)}) collective-permute-start(bf16[224,256]{1,0:T(8,128)(2,1)S(1)} %gate_up.5.refs_4_), channel_id=1, source_target_pairs={{0,2},{1,3},{2,0},{3,1},{4,6},{5,7},{6,4},{7,5},{8,10},{9,11},{10,... | collective-permute-start | bytes 344072 | tf_op jit(solution)/shard_map/ppermute | solution.py:201
  217.5 1.8 copy-start.2
  219.3 11.5 %copy-start.16 = (f32[1,64,3]{1,0,2:T(1,128)S(1)}, f32[1,64,3]{1,0,2:T(1,128)}, u32[]{:S(2)}) copy-start(f32[1,64,3]{1,0,2:T(1,128)} %param.10) | copy-start | bytes 2308
  219.3 92.3 %all-to-all-start.2 = ((bf16[128,8,1792]{2,1,0:T(8,128)(2,1)}), bf16[128,8,1792]{2,1,0:T(8,128)(2,1)}, u32[]{:S(2)}, u32[]{:S(2)}) async-start(bf16[128,8,1792]{2,1,0:T(8,128)(2,1)} %bitcast.54), calls=%async_computation.2 | async-start | bytes 7340032 | tf_op jit(solution)/shard_map/all_to_all | solution.py:204

commit v3 on v2

--- a/solution.py
+++ b/solution.py
@@ -253,9 +253,6 @@
     landed = [block.reshape(FOLD * slots, block.shape[2]) for block in landed]
     arrived = []
     for c in range(len(WIDTHS)):
-        if c > 0:
-            early = arrived[c - 1][2], arrived[c - 1][5]
-            landed[c] = lax.optimization_barrier((landed[c], *early))[0]
         first, second = unfold(landed[c], sort, half, 1)
         left_first, right_second = shift(first, 1), shift(second, -1)
         left_second, right_first = shift(second, 1), shift(first, -1)
@@ -265,9 +262,7 @@
         )
     state = None
     for c in range(len(WIDTHS) - 1):
-        early = arrived[c + 1][2], arrived[c + 1][5]
-        begun = list(lax.optimization_barrier((*arrived[c], *early))[: len(arrived[c])])
-        state = gate_up(begun, gate, up, firsts[c], state, 0, False)
+        state = gate_up(arrived[c], gate, up, firsts[c], state, 0, False)
     mine_near = gate_up(arrived[-1][:6], gate, up, firsts[-1], state, 0, True)
     near = [mine_near, shift(mine_near, 1), shift(mine_near, -1), shift(mine_near, 2)]
     mine_far = gate_up(arrived[-1][6:], gate, up, firsts[-1], state, 3, True)

time: 318 us -> 338 us (1.063)
  waiting for transfers between devices: 190 us -> 213 us
    ppermute x21, waiting for transfers between devices: 90 us -> 108 us  [shift(): return lax.ppermute(block, 'expert', route)]
    ppermute x21, starting transfers between devices: 31.1 us -> 23.7 us  [shift(): return lax.ppermute(block, 'expert', route)]
    all_to_all x3, waiting for transfers between devices: 100 us -> 106 us  [exchange(): lax.all_to_all(block, 'expert', split_axis=0, concat_axis=0, axis_index_g...]
    all_to_all x3, starting transfers between devices: 32.5 us -> 37 us  [exchange(): lax.all_to_all(block, 'expert', split_axis=0, concat_axis=0, axis_index_g...]
  transfers between devices with their start and end apart: 25 -> 25, of which waited for: 13 -> 11; matrix products, arithmetic and copies ran while one was open for 7% -> 6% of each run, Pallas kernels for 6% -> 5%
where the time goes in v3:
time: 338 us; the launch traced here: 337 us
  waiting for transfers between devices  213 us (63%)
  starting transfers between devices  60.7 us (18%)
  Pallas kernels  30.4 us (9%)
  local copies, waits for them, and re-layouts  22 us (7%)
  matrix products  5.12 us (2%)
  other arithmetic  4.5 us (1%)
    ppermute x21, waiting for transfers between devices, shift(): return lax.ppermute(block, 'expert', route)  108 us
    all_to_all x3, waiting for transfers between devices, exchange(): lax.all_to_all(block, 'expert', split_axis=0, concat_axis=0, axis_index_g...  106 us
    all_to_all x3, starting transfers between devices, exchange(): lax.all_to_all(block, 'expert', split_axis=0, concat_axis=0, axis_index_g...  37 us
    ppermute x21, starting transfers between devices, shift(): return lax.ppermute(block, 'expert', route)  23.7 us
    unnamed x50, local copies, waits for them, and re-layouts  13.4 us
    pallas_call x3, Pallas kernels, gate_up(): pl.pallas_call(functools.partial(gate_up_kernel, len(pieces), steps, last...  11.2 us
    pallas_call x1, Pallas kernels, down(): pl.pallas_call(functools.partial(down_kernel, orders), grid=(width // col...  7.63 us
  transfers between devices with their start and end apart: 25, of which 11 were waited for; matrix products, arithmetic and copies ran while one was open for 6% of the time, Pallas kernels for 5%

profile of v3, /device:TPU:32, one launch (start us, length us, event | category | flops | bytes accessed | tf_op | source)
XLA Modules:
  0.0 336.6 jit_solution(6634400758621711664)
XLA Ops:
  2.3 1.0 compare_reduce_fusion
  4.0 0.8 copy-done.12
  4.8 2.6 convolution_convert_fusion
  7.4 11.2 %all-to-all-start.1 = ((bf16[32,56,512]{2,1,0:T(8,128)(2,1)}), bf16[32,56,512]{2,1,0:T(8,128)(2,1)S(1)}, u32[]{:S(2)}, u32[]{:S(2)}) async-start(bf16[32,56,512]{2,1,0:T(8,128)(2,1)} %bitcast.56), calls=%async_computation.1 | async-start | bytes 3670016 | tf_op jit(solution)/shard_map/all_to_all | solution.py:204
  18.7 3.3 dynamic-slice_bitcast_fusion
  22.0 1.6 collective-permute-start.1
  23.5 1.7 collective-permute-start.2
  25.2 2.0 collective-permute-start.3
  28.0 0.8 slice_dynamic-update-slice_fusion.14
  28.8 0.8 slice_dynamic-update-slice_fusion.13
  29.6 0.8 slice_dynamic-update-slice_fusion.12
  30.4 0.8 slice_dynamic-update-slice_fusion.11
  33.7 2.5 convolution_convert_fusion.1
  36.2 9.2 %collective-permute-done.1.refs_9_ = bf16[256,1792]{1,0:T(8,128)(2,1)S(1)} collective-permute-done((bf16[256,1792]{1,0:T(8,128)(2,1)S(1)}, bf16[256,1792]{1,0:T(8,128)(2,1)S(1)}, u32[]{:S(2)}, u32[]{:S(2)}) %collective-permute-start.1) | collective-permute-done | bytes 917536 | tf_op jit(solution)/shard_map/ppermute | solution.py:201
  45.4 0.9 copy-done.6
  46.8 0.9 copy-done.8
  47.8 18.5 %collective-permute-done.3.refs_11_ = bf16[256,1792]{1,0:T(8,128)(2,1)S(1)} collective-permute-done((bf16[256,1792]{1,0:T(8,128)(2,1)S(1)}, bf16[256,1792]{1,0:T(8,128)(2,1)S(1)}, u32[]{:S(2)}, u32[]{:S(2)}) %collective-permute-start.3) | collective-permute-done | bytes 917536 | tf_op jit(solution)/shard_map/ppermute | solution.py:201
  66.3 0.9 copy-done.10
  67.2 9.8 %all-to-all-start = ((bf16[32,56,384]{2,1,0:T(8,128)(2,1)}), bf16[32,56,384]{2,1,0:T(8,128)(2,1)}, u32[]{:S(2)}, u32[]{:S(2)}) async-start(bf16[32,56,384]{2,1,0:T(8,128)(2,1)} %bitcast.57), calls=%async_computation | async-start | bytes 2752512 | tf_op jit(solution)/shard_map/all_to_all | solution.py:204
  77.4 3.2 unfold.3
  80.6 1.1 collective-permute-start.8
  81.7 2.1 collective-permute-start.11
  83.8 27.6 %all-to-all-done = bf16[32,56,384]{2,1,0:T(8,128)(2,1)} async-done(((bf16[32,56,384]{2,1,0:T(8,128)(2,1)}), bf16[32,56,384]{2,1,0:T(8,128)(2,1)}, u32[]{:S(2)}, u32[]{:S(2)}) %all-to-all-start) | async-done | bytes 1376288 | tf_op jit(solution)/shard_map/all_to_all | solution.py:204
  111.4 1.4 copy-done.4
  112.8 3.4 %unfold.2 = (bf16[112,3072]{1,0:T(8,128)(2,1)S(1)}, bf16[112,3072]{1,0:T(8,128)(2,1)S(1)}) custom-call(bf16[896,896]{1,0:T(8,128)(2,1)S(1)} %copy-done.4, bf16[1792,384]{1,0:T(8,128)(2,1)} %bitcast.9.landed_ref), custom_call_target="tpu_custom_call" | custom-call | flops 1233125376 | bytes 2752512 | tf_op jit(solution)/shard_map/unfold/pallas_call | solution.py:40
  116.3 1.1 collective-permute-start.4
  117.3 2.4 collective-permute-start.10
  119.8 16.3 %collective-permute-done.4.refs_2_ = bf16[112,3072]{1,0:T(8,128)(2,1)S(1)} collective-permute-done((bf16[112,3072]{1,0:T(8,128)(2,1)S(1)}, bf16[112,3072]{1,0:T(8,128)(2,1)S(1)}, u32[]{:S(2)}, u32[]{:S(2)}) %collective-permute-start.4) | collective-permute-done | bytes 688160 | tf_op jit(solution)/shard_map/ppermute | solution.py:201
  136.6 19.0 %collective-permute-done.7.refs_5_ = bf16[112,3072]{1,0:T(8,128)(2,1)S(1)} collective-permute-done((bf16[112,3072]{1,0:T(8,128)(2,1)S(1)}, bf16[112,3072]{1,0:T(8,128)(2,1)S(1)}, u32[]{:S(2)}, u32[]{:S(2)}) %collective-permute-start.7) | collective-permute-done | bytes 688160 | tf_op jit(solution)/shard_map/ppermute | solution.py:201
  155.9 3.4 collective-permute-start.18
  159.2 16.2 %collective-permute-done.12.refs_6_ = bf16[112,4096]{1,0:T(8,128)(2,1)S(1)} collective-permute-done((bf16[112,4096]{1,0:T(8,128)(2,1)S(1)}, bf16[112,4096]{1,0:T(8,128)(2,1)S(1)}, u32[]{:S(2)}, u32[]{:S(2)}) %collective-permute-start.12) | collective-permute-done | bytes 917536 | tf_op jit(solution)/shard_map/ppermute | solution.py:201
  175.8 6.4 %gate_up.3.refs_8_.refs_4_ = f32[896,512]{1,0:T(8,128)S(1)} custom-call(bf16[112,4096]{1,0:T(8,128)(2,1)} %get-tuple-element.17.refs_0_, bf16[112,4096]{1,0:T(8,128)(2,1)} %get-tuple-element.18.refs_1_, bf16[112,4096]{1,0:T(8,128)(2,1)S(1)} %collective-permute-done.8.refs_2_, bf16[112,4096]{1,0:T(8,128)(2,1)S(1)} %collective-permute-done.9.refs_3_, ...), custom_call_target="tpu_custom_call" | custom-call | flops 3758096384 | bytes 11534336 | tf_op jit(solution)/shard_map/gate_up/pallas_call | solution.py:89
  182.3 7.9 %collective-permute-done.17.refs_0_ = bf16[112,3072]{1,0:T(8,128)(2,1)S(1)} collective-permute-done((bf16[112,3072]{1,0:T(8,128)(2,1)S(1)}, bf16[112,3072]{1,0:T(8,128)(2,1)S(1)}, u32[]{:S(2)}, u32[]{:S(2)}) %collective-permute-start.17) | collective-permute-done | bytes 688160 | tf_op jit(solution)/shard_map/ppermute | solution.py:201
  190.2 1.5 gate_up.5.refs_4_
  191.9 10.2 %collective-permute-done.5.refs_3_ = bf16[112,3072]{1,0:T(8,128)(2,1)S(1)} collective-permute-done((bf16[112,3072]{1,0:T(8,128)(2,1)S(1)}, bf16[112,3072]{1,0:T(8,128)(2,1)S(1)}, u32[]{:S(2)}, u32[]{:S(2)}) %collective-permute-start.5) | collective-permute-done | bytes 688160 | tf_op jit(solution)/shard_map/ppermute | solution.py:201
  202.1 3.3 gate_up.4.refs_0_
  205.5 3.2 collective-permute-start.15
  208.9 1.5 collective-permute-start.20
  210.4 2.1 collective-permute-start.21
  213.2 9.9 %collective-permute-done.20.refs_6_ = bf16[224,256]{1,0:T(8,128)(2,1)S(1)} collective-permute-done((bf16[224,256]{1,0:T(8,128)(2,1)S(1)}, bf16[224,256]{1,0:T(8,128)(2,1)S(1)}, u32[]{:S(2)}, u32[]{:S(2)}) %collective-permute-start.20) | collective-permute-done | bytes 114720 | tf_op jit(solution)/shard_map/ppermute | solution.py:201
  223.1 7.6 %down.1 = bf16[1024,1792]{1,0:T(8,128)(2,1)S(1)} custom-call(bf16[672,256]{1,0:T(8,128)(2,1)S(1)} %gate_up.4.refs_0_, bf16[672,256]{1,0:T(8,128)(2,1)S(1)} %collective-permute-done.14.refs_1_, bf16[672,256]{1,0:T(8,128)(2,1)S(1)} %collective-permute-done.15.refs_2_, bf16[672,256]{1,0:T(8,128)(2,1)S(1)} %collective-permute-done.16.refs_3_, ...), custom_call_target="tpu_custom_call" | custom-call | flops 5637144576 | bytes 7340032 | tf_op jit(solution)/shard_map/down/pallas_call | solution.py:134
  230.7 1.8 copy-done.2
  232.6 16.0 %all-to-all-start.2 = ((bf16[128,8,1792]{2,1,0:T(8,128)(2,1)}), bf16[128,8,1792]{2,1,0:T(8,128)(2,1)}, u32[]{:S(2)}, u32[]{:S(2)}) async-start(bf16[128,8,1792]{2,1,0:T(8,128)(2,1)} %bitcast.54), calls=%async_computation.2 | async-start | bytes 7340032 | tf_op jit(solution)/shard_map/all_to_all | solution.py:204
  249.0 0.8 broadcast_select_fusion
  249.9 2.1 select_n.187
  252.0 1.5 copy.26.mixing_ref
  253.5 78.2 %all-to-all-done.2 = bf16[128,8,1792]{2,1,0:T(8,128)(2,1)} async-done(((bf16[128,8,1792]{2,1,0:T(8,128)(2,1)}), bf16[128,8,1792]{2,1,0:T(8,128)(2,1)}, u32[]{:S(2)}, u32[]{:S(2)}) %all-to-all-start.2) | async-done | bytes 3670048 | tf_op jit(solution)/shard_map/all_to_all | solution.py:204
  331.7 5.0 %mix.1 = bf16[64,7168]{1,0:T(8,128)(2,1)} custom-call(bf16[1024,1792]{1,0:T(8,128)(2,1)} %bitcast.15.returned_ref, bf16[512,1024]{1,0:T(8,128)(2,1)S(1)} %copy.26.mixing_ref, bf16[64,7168]{1,0:T(8,128)(2,1)S(1)} %bitcast.53), custom_call_target="tpu_custom_call" | custom-call | tf_op jit(solution)/shard_map/mix/pallas_call | solution.py:170
  (98 shorter events, 9.7 us)
Async XLA Ops:
  0.0 3.6 %copy-start.15 = (f32[1,7168]{1,0:T(1,128)S(1)}, f32[1,7168]{1,0:T(1,128)}, u32[]{:S(2)}) copy-start(f32[1,7168]{1,0:T(1,128)} %param.8) | copy-start | bytes 86020
  0.0 3.3 collective-permute-start
  3.3 4.1 %copy-start.13 = (pred[1792,512]{1,0:T(8,128)(4,1)}, pred[1792,512]{1,0:T(8,128)(4,1)S(1)}, u32[]{:S(2)}) copy-start(pred[1792,512]{1,0:T(8,128)(4,1)S(1)} %compare_reduce_fusion) | copy-start | bytes 2752516
  3.9 0.9 copy-start.12
  7.4 59.8 %all-to-all-start.1 = ((bf16[32,56,512]{2,1,0:T(8,128)(2,1)}), bf16[32,56,512]{2,1,0:T(8,128)(2,1)S(1)}, u32[]{:S(2)}, u32[]{:S(2)}) async-start(bf16[32,56,512]{2,1,0:T(8,128)(2,1)} %bitcast.56), calls=%async_computation.1 | async-start | bytes 3670016 | tf_op jit(solution)/shard_map/all_to_all | solution.py:204
  18.7 15.0 %copy-start.14 = (pred[1792,512]{1,0:T(8,128)(4,1)S(1)}, pred[1792,512]{1,0:T(8,128)(4,1)}, u32[]{:S(2)}) copy-start(pred[1792,512]{1,0:T(8,128)(4,1)} %copy-done.13) | copy-start | bytes 2752516
  22.0 23.5 %collective-permute-start.1 = (bf16[256,1792]{1,0:T(8,128)(2,1)S(1)}, bf16[256,1792]{1,0:T(8,128)(2,1)S(1)}, u32[]{:S(2)}, u32[]{:S(2)}) collective-permute-start(bf16[256,1792]{1,0:T(8,128)(2,1)S(1)} %get-tuple-element.24), channel_id=1, source_target_pairs={{0,1},{1,2},{2,3},{3,0},{4,5},{5,6},{6,7},{7,4},{8,9},{9,10},{10,1... | collective-permute-start | bytes 2752520 | tf_op jit(solution)/shard_map/ppermute | solution.py:201
  23.5 23.3 %collective-permute-start.2 = (bf16[256,1792]{1,0:T(8,128)(2,1)S(1)}, bf16[256,1792]{1,0:T(8,128)(2,1)S(1)}, u32[]{:S(2)}, u32[]{:S(2)}) collective-permute-start(bf16[256,1792]{1,0:T(8,128)(2,1)S(1)} %get-tuple-element.26), channel_id=1, source_target_pairs={{0,3},{1,0},{2,1},{3,2},{4,7},{5,4},{6,5},{7,6},{8,11},{9,8},{10,9... | collective-permute-start | bytes 2752520 | tf_op jit(solution)/shard_map/ppermute | solution.py:201
  25.2 41.1 %collective-permute-start.3 = (bf16[256,1792]{1,0:T(8,128)(2,1)S(1)}, bf16[256,1792]{1,0:T(8,128)(2,1)S(1)}, u32[]{:S(2)}, u32[]{:S(2)}) collective-permute-start(bf16[256,1792]{1,0:T(8,128)(2,1)S(1)} %get-tuple-element.23), channel_id=1, source_target_pairs={{0,2},{1,3},{2,0},{3,1},{4,6},{5,7},{6,4},{7,5},{8,10},{9,11},{10,... | collective-permute-start | bytes 2752520 | tf_op jit(solution)/shard_map/ppermute | solution.py:201
  45.4 0.9 copy-start.6
  46.8 0.9 copy-start.8
  66.3 0.9 copy-start.10
  67.2 44.2 %all-to-all-start = ((bf16[32,56,384]{2,1,0:T(8,128)(2,1)}), bf16[32,56,384]{2,1,0:T(8,128)(2,1)}, u32[]{:S(2)}, u32[]{:S(2)}) async-start(bf16[32,56,384]{2,1,0:T(8,128)(2,1)} %bitcast.57), calls=%async_computation | async-start | bytes 2752512 | tf_op jit(solution)/shard_map/all_to_all | solution.py:204
  77.4 3.2 copy-start.3
  80.6 39.2 %collective-permute-start.8 = (bf16[112,4096]{1,0:T(8,128)(2,1)}, bf16[112,4096]{1,0:T(8,128)(2,1)S(1)}, u32[]{:S(2)}, u32[]{:S(2)}) collective-permute-start(bf16[112,4096]{1,0:T(8,128)(2,1)} %get-tuple-element.17.refs_0_), channel_id=1, source_target_pairs={{0,1},{1,2},{2,3},{3,0},{4,5},{5,6},{6,7},{7,4},{8,9},{9,10},{10,1... | collective-permute-start | bytes 2752520 | tf_op jit(solution)/shard_map/ppermute | solution.py:201
  81.7 54.8 %collective-permute-start.11 = (bf16[112,4096]{1,0:T(8,128)(2,1)}, bf16[112,4096]{1,0:T(8,128)(2,1)S(1)}, u32[]{:S(2)}, u32[]{:S(2)}) collective-permute-start(bf16[112,4096]{1,0:T(8,128)(2,1)} %get-tuple-element.18.refs_1_), channel_id=1, source_target_pairs={{0,3},{1,0},{2,1},{3,2},{4,7},{5,4},{6,5},{7,6},{8,11},{9,8},{10,9... | collective-permute-start | bytes 2752520 | tf_op jit(solution)/shard_map/ppermute | solution.py:201
  111.4 1.4 copy-start.4
  112.8 63.0 %copy-start = (bf16[1,7168,256]{2,1,0:T(8,128)(2,1)S(1)}, bf16[1,7168,256]{2,1,0:T(8,128)(2,1)}, u32[]{:S(2)}) copy-start(bf16[1,7168,256]{2,1,0:T(8,128)(2,1)} %param.11) | copy-start | bytes 11010052
  116.3 19.8 %collective-permute-start.4 = (bf16[112,3072]{1,0:T(8,128)(2,1)S(1)}, bf16[112,3072]{1,0:T(8,128)(2,1)S(1)}, u32[]{:S(2)}, u32[]{:S(2)}) collective-permute-start(bf16[112,3072]{1,0:T(8,128)(2,1)S(1)} %get-tuple-element.15.refs_0_), channel_id=1, source_target_pairs={{0,1},{1,2},{2,3},{3,0},{4,5},{5,6},{6,7},{7,4},{8,9},{9,10},{10,1... | collective-permute-start | bytes 2064392 | tf_op jit(solution)/shard_map/ppermute | solution.py:201
  117.3 38.5 %collective-permute-start.10 = (bf16[112,4096]{1,0:T(8,128)(2,1)}, bf16[112,4096]{1,0:T(8,128)(2,1)S(1)}, u32[]{:S(2)}, u32[]{:S(2)}) collective-permute-start(bf16[112,4096]{1,0:T(8,128)(2,1)} %get-tuple-element.17.refs_0_), channel_id=1, source_target_pairs={{0,3},{1,0},{2,1},{3,2},{4,7},{5,4},{6,5},{7,6},{8,11},{9,8},{10,9... | collective-permute-start | bytes 2752520 | tf_op jit(solution)/shard_map/ppermute | solution.py:201
  119.8 39.5 %collective-permute-start.9 = (bf16[112,4096]{1,0:T(8,128)(2,1)}, bf16[112,4096]{1,0:T(8,128)(2,1)S(1)}, u32[]{:S(2)}, u32[]{:S(2)}) collective-permute-start(bf16[112,4096]{1,0:T(8,128)(2,1)} %get-tuple-element.18.refs_1_), channel_id=1, source_target_pairs={{0,1},{1,2},{2,3},{3,0},{4,5},{5,6},{6,7},{7,4},{8,9},{9,10},{10,1... | collective-permute-start | bytes 2752520 | tf_op jit(solution)/shard_map/ppermute | solution.py:201
  119.8 55.7 %collective-permute-start.12 = (bf16[112,4096]{1,0:T(8,128)(2,1)S(1)}, bf16[112,4096]{1,0:T(8,128)(2,1)S(1)}, u32[]{:S(2)}, u32[]{:S(2)}) collective-permute-start(bf16[112,4096]{1,0:T(8,128)(2,1)S(1)} %collective-permute-done.8.refs_2_), channel_id=1, source_target_pairs={{0,1},{1,2},{2,3},{3,0},{4,5},{5,6},{6,7},{7,4},{8,9},{9,10},{10,1... | collective-permute-start | bytes 2752520 | tf_op jit(solution)/shard_map/ppermute | solution.py:201
  136.1 19.5 %collective-permute-start.7 = (bf16[112,3072]{1,0:T(8,128)(2,1)S(1)}, bf16[112,3072]{1,0:T(8,128)(2,1)S(1)}, u32[]{:S(2)}, u32[]{:S(2)}) collective-permute-start(bf16[112,3072]{1,0:T(8,128)(2,1)S(1)} %get-tuple-element.16.refs_1_), channel_id=1, source_target_pairs={{0,3},{1,0},{2,1},{3,2},{4,7},{5,4},{6,5},{7,6},{8,11},{9,8},{10,9... | collective-permute-start | bytes 2064392 | tf_op jit(solution)/shard_map/ppermute | solution.py:201
  136.5 39.3 %collective-permute-start.13 = (bf16[112,4096]{1,0:T(8,128)(2,1)S(1)}, bf16[112,4096]{1,0:T(8,128)(2,1)S(1)}, u32[]{:S(2)}, u32[]{:S(2)}) collective-permute-start(bf16[112,4096]{1,0:T(8,128)(2,1)S(1)} %collective-permute-done.11.refs_5_), channel_id=1, source_target_pairs={{0,3},{1,0},{2,1},{3,2},{4,7},{5,4},{6,5},{7,6},{8,11},{9,8},{10,9... | collective-permute-start | bytes 2752520 | tf_op jit(solution)/shard_map/ppermute | solution.py:201
  155.6 34.6 %collective-permute-start.17 = (bf16[112,3072]{1,0:T(8,128)(2,1)S(1)}, bf16[112,3072]{1,0:T(8,128)(2,1)S(1)}, u32[]{:S(2)}, u32[]{:S(2)}) collective-permute-start(bf16[112,3072]{1,0:T(8,128)(2,1)S(1)} %collective-permute-done.4.refs_2_), channel_id=1, source_target_pairs={{0,1},{1,2},{2,3},{3,0},{4,5},{5,6},{6,7},{7,4},{8,9},{9,10},{10,1... | collective-permute-start | bytes 2064392 | tf_op jit(solution)/shard_map/ppermute | solution.py:201
  155.9 34.3 %collective-permute-start.18 = (bf16[112,3072]{1,0:T(8,128)(2,1)S(1)}, bf16[112,3072]{1,0:T(8,128)(2,1)S(1)}, u32[]{:S(2)}, u32[]{:S(2)}) collective-permute-start(bf16[112,3072]{1,0:T(8,128)(2,1)S(1)} %collective-permute-done.7.refs_5_), channel_id=1, source_target_pairs={{0,3},{1,0},{2,1},{3,2},{4,7},{5,4},{6,5},{7,6},{8,11},{9,8},{10,9... | collective-permute-start | bytes 2064392 | tf_op jit(solution)/shard_map/ppermute | solution.py:201
  159.2 42.8 %collective-permute-start.5 = (bf16[112,3072]{1,0:T(8,128)(2,1)S(1)}, bf16[112,3072]{1,0:T(8,128)(2,1)S(1)}, u32[]{:S(2)}, u32[]{:S(2)}) collective-permute-start(bf16[112,3072]{1,0:T(8,128)(2,1)S(1)} %get-tuple-element.16.refs_1_), channel_id=1, source_target_pairs={{0,1},{1,2},{2,3},{3,0},{4,5},{5,6},{6,7},{7,4},{8,9},{9,10},{10,1... | collective-permute-start | bytes 2064392 | tf_op jit(solution)/shard_map/ppermute | solution.py:201
  175.4 26.6 %collective-permute-start.6 = (bf16[112,3072]{1,0:T(8,128)(2,1)S(1)}, bf16[112,3072]{1,0:T(8,128)(2,1)S(1)}, u32[]{:S(2)}, u32[]{:S(2)}) collective-permute-start(bf16[112,3072]{1,0:T(8,128)(2,1)S(1)} %get-tuple-element.15.refs_0_), channel_id=1, source_target_pairs={{0,3},{1,0},{2,1},{3,2},{4,7},{5,4},{6,5},{7,6},{8,11},{9,8},{10,9... | collective-permute-start | bytes 2064392 | tf_op jit(solution)/shard_map/ppermute | solution.py:201
  175.8 14.4 %copy-start.1 = (bf16[1,7168,256]{2,1,0:T(8,128)(2,1)S(1)}, bf16[1,7168,256]{2,1,0:T(8,128)(2,1)}, u32[]{:S(2)}) copy-start(bf16[1,7168,256]{2,1,0:T(8,128)(2,1)} %param.12) | copy-start | bytes 11010052
  191.7 31.4 %copy-start.5 = (bf16[256,1792]{1,0:T(8,128)(2,1)S(1)}, bf16[256,1792]{1,0:T(8,128)(2,1)}, u32[]{:S(2)}) copy-start(bf16[256,1792]{1,0:T(8,128)(2,1)} %get-tuple-element.19.refs_8_) | copy-start | bytes 2752516
  191.7 31.4 %copy-start.7 = (bf16[256,1792]{1,0:T(8,128)(2,1)S(1)}, bf16[256,1792]{1,0:T(8,128)(2,1)}, u32[]{:S(2)}) copy-start(bf16[256,1792]{1,0:T(8,128)(2,1)} %copy-done.6) | copy-start | bytes 2752516
  191.7 31.4 %copy-start.9 = (bf16[256,1792]{1,0:T(8,128)(2,1)S(1)}, bf16[256,1792]{1,0:T(8,128)(2,1)}, u32[]{:S(2)}) copy-start(bf16[256,1792]{1,0:T(8,128)(2,1)} %copy-done.8) | copy-start | bytes 2752516
  191.7 31.4 %copy-start.11 = (bf16[256,1792]{1,0:T(8,128)(2,1)S(1)}, bf16[256,1792]{1,0:T(8,128)(2,1)}, u32[]{:S(2)}) copy-start(bf16[256,1792]{1,0:T(8,128)(2,1)} %copy-done.10) | copy-start | bytes 2752516
  191.7 18.6 %collective-permute-start.19 = (bf16[224,256]{1,0:T(8,128)(2,1)S(1)}, bf16[224,256]{1,0:T(8,128)(2,1)S(1)}, u32[]{:S(2)}, u32[]{:S(2)}) collective-permute-start(bf16[224,256]{1,0:T(8,128)(2,1)S(1)} %gate_up.5.refs_4_), channel_id=1, source_target_pairs={{0,1},{1,2},{2,3},{3,0},{4,5},{5,6},{6,7},{7,4},{8,9},{9,10},{10,1... | collective-permute-start | bytes 344072 | tf_op jit(solution)/shard_map/ppermute | solution.py:201
  205.4 17.7 %collective-permute-start.14 = (bf16[672,256]{1,0:T(8,128)(2,1)S(1)}, bf16[672,256]{1,0:T(8,128)(2,1)S(1)}, u32[]{:S(2)}, u32[]{:S(2)}) collective-permute-start(bf16[672,256]{1,0:T(8,128)(2,1)S(1)} %gate_up.4.refs_0_), channel_id=1, source_target_pairs={{0,1},{1,2},{2,3},{3,0},{4,5},{5,6},{6,7},{7,4},{8,9},{9,10},{10,1... | collective-permute-start | bytes 1032200 | tf_op jit(solution)/shard_map/ppermute | solution.py:201
  205.5 17.6 %collective-permute-start.15 = (bf16[672,256]{1,0:T(8,128)(2,1)S(1)}, bf16[672,256]{1,0:T(8,128)(2,1)S(1)}, u32[]{:S(2)}, u32[]{:S(2)}) collective-permute-start(bf16[672,256]{1,0:T(8,128)(2,1)S(1)} %gate_up.4.refs_0_), channel_id=1, source_target_pairs={{0,3},{1,0},{2,1},{3,2},{4,7},{5,4},{6,5},{7,6},{8,11},{9,8},{10,9... | collective-permute-start | bytes 1032200 | tf_op jit(solution)/shard_map/ppermute | solution.py:201
  208.7 14.4 %collective-permute-start.16 = (bf16[672,256]{1,0:T(8,128)(2,1)S(1)}, bf16[672,256]{1,0:T(8,128)(2,1)S(1)}, u32[]{:S(2)}, u32[]{:S(2)}) collective-permute-start(bf16[672,256]{1,0:T(8,128)(2,1)S(1)} %gate_up.4.refs_0_), channel_id=1, source_target_pairs={{0,2},{1,3},{2,0},{3,1},{4,6},{5,7},{6,4},{7,5},{8,10},{9,11},{10,... | collective-permute-start | bytes 1032200 | tf_op jit(solution)/shard_map/ppermute | solution.py:201
  208.9 14.1 %collective-permute-start.20 = (bf16[224,256]{1,0:T(8,128)(2,1)S(1)}, bf16[224,256]{1,0:T(8,128)(2,1)S(1)}, u32[]{:S(2)}, u32[]{:S(2)}) collective-permute-start(bf16[224,256]{1,0:T(8,128)(2,1)S(1)} %gate_up.5.refs_4_), channel_id=1, source_target_pairs={{0,3},{1,0},{2,1},{3,2},{4,7},{5,4},{6,5},{7,6},{8,11},{9,8},{10,9... | collective-permute-start | bytes 344072 | tf_op jit(solution)/shard_map/ppermute | solution.py:201
  210.4 12.7 %collective-permute-start.21 = (bf16[224,256]{1,0:T(8,128)(2,1)S(1)}, bf16[224,256]{1,0:T(8,128)(2,1)S(1)}, u32[]{:S(2)}, u32[]{:S(2)}) collective-permute-start(bf16[224,256]{1,0:T(8,128)(2,1)S(1)} %gate_up.5.refs_4_), channel_id=1, source_target_pairs={{0,2},{1,3},{2,0},{3,1},{4,6},{5,7},{6,4},{7,5},{8,10},{9,11},{10,... | collective-permute-start | bytes 344072 | tf_op jit(solution)/shard_map/ppermute | solution.py:201
  230.7 1.8 copy-start.2
  232.6 16.0 %copy-start.16 = (f32[1,64,3]{1,0,2:T(1,128)S(1)}, f32[1,64,3]{1,0,2:T(1,128)}, u32[]{:S(2)}) copy-start(f32[1,64,3]{1,0,2:T(1,128)} %param.10) | copy-start | bytes 2308
  232.6 99.1 %all-to-all-start.2 = ((bf16[128,8,1792]{2,1,0:T(8,128)(2,1)}), bf16[128,8,1792]{2,1,0:T(8,128)(2,1)}, u32[]{:S(2)}, u32[]{:S(2)}) async-start(bf16[128,8,1792]{2,1,0:T(8,128)(2,1)} %bitcast.54), calls=%async_computation.2 | async-start | bytes 7340032 | tf_op jit(solution)/shard_map/all_to_all | solution.py:204
